TPU v7x, 32 devices: a whole 2x2x4 slice. The times are simulated.
32 devices in a mesh: dp: 4 (over y, x), tensor: 8 (over z, core).
Axes of the slice: x: 2, y: 2, z: 4, core: 2. Of those that a mesh axis runs over, the one named last changes fastest.
Arguments:
- tokens: float32 [13824, 1024], P(('dp', 'tensor')), may hold values from -6 to 6
- cotangent: float32 [13824, 1024], P(('dp', 'tensor')), may hold values from -6 to 6
- vectors: float32 [6, 1024], replicated, may hold values from -0.9 to 1.9, as said below
- vectors_m: float32 [6, 1024], replicated, may hold values from -80 to 80
- vectors_v: float32 [6, 1024], replicated, may hold values from 6.912 to 110.592
- w_qkv: float32 [1024, 3072], P('dp', 'tensor'), may hold values from -0.25 to 0.25
- qkv_m: float32 [1024, 3072], P('dp', 'tensor'), may hold values from -80 to 80
- qkv_v: float32 [1024, 3072], P('dp', 'tensor'), may hold values from 6.912 to 110.592
- w_out: float32 [1024, 1024], P('tensor', 'dp'), may hold values from -0.5 to 0.5
- out_m: float32 [1024, 1024], P('tensor', 'dp'), may hold values from -32 to 32
- out_v: float32 [1024, 1024], P('tensor', 'dp'), may hold values from 1.10592 to 17.69472
- w_up: float32 [1024, 4096], P('dp', 'tensor'), may hold values from -0.1875 to 0.1875
- up_m: float32 [1024, 4096], P('dp', 'tensor'), may hold values from -24 to 24
- up_v: float32 [1024, 4096], P('dp', 'tensor'), may hold values from 0.62208 to 9.95328
- hidden_bias: float32 [4096], P('tensor'), may hold values from -3 to 3
- bias_m: float32 [4096], P('tensor'), may hold values from -24 to 24
- bias_v: float32 [4096], P('tensor'), may hold values from 0.62208 to 9.95328
- w_down: float32 [4096, 1024], P('tensor', 'dp'), may hold values from -0.09375 to 0.09375
- down_m: float32 [4096, 1024], P('tensor', 'dp'), may hold values from -48 to 48
- down_v: float32 [4096, 1024], P('tensor', 'dp'), may hold values from 2.48832 to 39.81312
Outputs:
- output: float32 [13824, 1024], P(('dp', 'tensor'))
- input_grad: float32 [13824, 1024], P(('dp', 'tensor'))
- vectors_grad: float32 [6, 1024], replicated
- vectors_m_new: float32 [6, 1024], replicated
- vectors_v_new: float32 [6, 1024], replicated
- vectors_new: float32 [6, 1024], replicated
- qkv_grad: float32 [1024, 3072], P('dp', 'tensor')
- qkv_m_new: float32 [1024, 3072], P('dp', 'tensor')
- qkv_v_new: float32 [1024, 3072], P('dp', 'tensor')
- qkv_new: float32 [1024, 3072], P('dp', 'tensor')
- out_grad: float32 [1024, 1024], P('tensor', 'dp')
- out_m_new: float32 [1024, 1024], P('tensor', 'dp')
- out_v_new: float32 [1024, 1024], P('tensor', 'dp')
- out_new: float32 [1024, 1024], P('tensor', 'dp')
- up_grad: float32 [1024, 4096], P('dp', 'tensor')
- up_m_new: float32 [1024, 4096], P('dp', 'tensor')
- up_v_new: float32 [1024, 4096], P('dp', 'tensor')
- up_new: float32 [1024, 4096], P('dp', 'tensor')
- bias_grad: float32 [4096], P('tensor')
- bias_m_new: float32 [4096], P('tensor')
- bias_v_new: float32 [4096], P('tensor')
- bias_new: float32 [4096], P('tensor')
- down_grad: float32 [4096, 1024], P('tensor', 'dp')
- down_m_new: float32 [4096, 1024], P('tensor', 'dp')
- down_v_new: float32 [4096, 1024], P('tensor', 'dp')
- down_new: float32 [4096, 1024], P('tensor', 'dp')
Inputs may be any that keep to these rules, and one draw needn't show every extreme that they name: `vectors`: rows 0 and 2 lie within 1 - 0.9 to 1 + 0.9, the other rows within -0.9 to 0.9.
All inputs are finite; a program needn't handle non-finite values.
Results may differ from a plain program's by a relative error of at most 0.018.
Values may be sent and summed in bfloat16 or wider, within the bound.
No kernel may reach another device: no remote copies, remote signals or barrier semaphores. Data moves between devices by JAX's collectives and lax.ppermute only.
A program may use at most 192 MiB of HBM per device.

v0:
```python
import math

import jax
import jax.numpy as jnp
from jax import lax
from jax.sharding import PartitionSpec as P

HD = 64
FF = 4096
SEQ = 576
STEP = 10


def layer_norm(rows_in, gain, shift):
    centred = rows_in - jnp.mean(rows_in, axis=-1, keepdims=True)
    spread = jnp.mean(centred * centred, axis=-1, keepdims=True)
    return centred * lax.rsqrt(spread + 1e-06) * gain + shift


def matmul(left, right):
    return jnp.dot(left, right, preferred_element_type=jnp.float32)


def inner_rows(left, right):
    return lax.dot_general(
        left, right, (((0,), (0,)), ((), ())), preferred_element_type=jnp.float32
    )


def outer_cols(left, right):
    return lax.dot_general(
        left, right, (((1,), (1,)), ((), ())), preferred_element_type=jnp.float32
    )


def exact_gelu(values):
    return jax.nn.gelu(values, approximate=False)


def adam_step(weight, gradient, first, second, rate, decay):
    first = 0.9 * first + 0.1 * gradient
    second = 0.999 * second + 0.001 * gradient * gradient
    first_fix = 1.0 - 0.9**STEP
    second_fix = 1.0 - 0.999**STEP
    update = first / first_fix / (jnp.sqrt(second / second_fix) + 1e-08) + decay * weight
    return (gradient, first, second, weight - rate * update)


def per_device(
    tokens,
    cotangent,
    vectors,
    vectors_m,
    vectors_v,
    w_qkv,
    qkv_m,
    qkv_v,
    w_out,
    out_m,
    out_v,
    w_up,
    up_m,
    up_v,
    hidden_bias,
    bias_m,
    bias_v,
    w_down,
    down_m,
    down_v,
):
    heads_here = w_qkv.shape[1] // (3 * HD)
    scale = 1.0 / math.sqrt(HD)
    qkv_full, out_full, up_full, down_full = (
        lax.all_gather(w_qkv.astype(jnp.bfloat16), "dp", axis=0, tiled=True),
        lax.all_gather(w_out.astype(jnp.bfloat16), "dp", axis=1, tiled=True),
        lax.all_gather(w_up.astype(jnp.bfloat16), "dp", axis=0, tiled=True),
        lax.all_gather(w_down.astype(jnp.bfloat16), "dp", axis=1, tiled=True),
    )
    normed_one = layer_norm(tokens, vectors[0], vectors[1])
    gathered_one = lax.all_gather(normed_one.astype(jnp.bfloat16), "tensor", axis=0, tiled=True)
    group_size = gathered_one.shape[0]
    images = group_size // SEQ
    qkv_low = matmul(gathered_one, qkv_full).astype(jnp.bfloat16)
    qkv_images = qkv_low.reshape(images, SEQ, heads_here, 3, HD)

    def attend_one(image_block):
        query_rows = image_block[:, :, 0]
        key_rows = image_block[:, :, 1]
        value_rows = image_block[:, :, 2]
        scores = (
            jnp.einsum("qhd,khd->hqk", query_rows, key_rows, preferred_element_type=jnp.float32)
            * scale
        )
        row_max = jnp.max(scores, axis=-1, keepdims=True)
        raised = jnp.exp(scores - row_max)
        denominator = jnp.sum(raised, axis=-1, keepdims=True)
        soft = raised / denominator
        mixed_out = jnp.einsum(
            "hqk,khd->qhd",
            soft.astype(jnp.bfloat16),
            value_rows,
            preferred_element_type=jnp.float32,
        )
        return (
            mixed_out.astype(jnp.bfloat16).reshape(SEQ, heads_here * HD),
            (row_max + jnp.log(denominator))[..., 0],
        )

    attended, log_totals = lax.map(attend_one, qkv_images)
    attended_flat = attended.reshape(group_size, heads_here * HD)
    head_rows = lax.all_to_all(attended_flat, "tensor", split_axis=0, concat_axis=1, tiled=True)
    out_all = lax.all_gather(out_full, "tensor", axis=0, tiled=True)
    attn_part = matmul(head_rows, out_all)
    middle = tokens + attn_part + vectors[4]
    normed_two = layer_norm(middle, vectors[2], vectors[3])
    gathered_two = lax.all_gather(normed_two.astype(jnp.bfloat16), "tensor", axis=0, tiled=True)
    hidden_pre = matmul(gathered_two, up_full) + hidden_bias
    hidden_low = exact_gelu(hidden_pre).astype(jnp.bfloat16)
    mlp_part = lax.psum_scatter(
        matmul(hidden_low, down_full).astype(jnp.bfloat16),
        "tensor",
        scatter_dimension=0,
        tiled=True,
    ).astype(jnp.float32)
    output = middle + mlp_part + vectors[5]
    grad_rows = lax.all_gather(cotangent.astype(jnp.bfloat16), "tensor", axis=0, tiled=True)
    down_part = inner_rows(hidden_low, grad_rows)
    hidden_grad = outer_cols(grad_rows, down_full)
    gelu_value, gelu_pull = jax.vjp(exact_gelu, hidden_pre)
    (pre_grad,) = gelu_pull(hidden_grad)
    bias_part = jnp.sum(pre_grad, axis=0)
    pre_low = pre_grad.astype(jnp.bfloat16)
    up_part = inner_rows(gathered_two, pre_low)
    normed_two_grad = lax.psum_scatter(
        outer_cols(pre_low, up_full), "tensor", scatter_dimension=0, tiled=True
    )
    norm_value, norm_two_pull = jax.vjp(layer_norm, middle, vectors[2], vectors[3])
    middle_part, gain_two, shift_two = norm_two_pull(normed_two_grad)
    middle_grad = cotangent + middle_part
    middle_rows = lax.all_gather(middle_grad.astype(jnp.bfloat16), "tensor", axis=0, tiled=True)
    out_part = inner_rows(attended_flat, middle_rows)
    attended_grad = outer_cols(middle_rows, out_full).astype(jnp.bfloat16)

    def attend_back(item_parts):
        image_block, log_total, grad_block = item_parts
        query_rows = image_block[:, :, 0]
        key_rows = image_block[:, :, 1]
        value_rows = image_block[:, :, 2]
        scores = (
            jnp.einsum("qhd,khd->hqk", query_rows, key_rows, preferred_element_type=jnp.float32)
            * scale
        )
        soft = jnp.exp(scores - log_total[..., None])
        grad_heads = grad_block.reshape(SEQ, heads_here, HD)
        soft_grad = jnp.einsum(
            "qhd,khd->hqk", grad_heads, value_rows, preferred_element_type=jnp.float32
        )
        row_dot = jnp.sum(soft_grad * soft, axis=-1, keepdims=True)
        score_grad = (soft * (soft_grad - row_dot)).astype(jnp.bfloat16)
        query_grad = (
            jnp.einsum("hqk,khd->qhd", score_grad, key_rows, preferred_element_type=jnp.float32)
            * scale
        )
        key_grad = (
            jnp.einsum("hqk,qhd->khd", score_grad, query_rows, preferred_element_type=jnp.float32)
            * scale
        )
        value_grad = jnp.einsum(
            "hqk,qhd->khd",
            soft.astype(jnp.bfloat16),
            grad_heads,
            preferred_element_type=jnp.float32,
        )
        joined = jnp.stack([query_grad, key_grad, value_grad], axis=2)
        return joined.astype(jnp.bfloat16).reshape(SEQ, heads_here * 3 * HD)

    qkv_back = lax.map(
        attend_back, (qkv_images, log_totals, attended_grad.reshape(images, SEQ, heads_here * HD))
    )
    qkv_back = qkv_back.reshape(group_size, heads_here * 3 * HD)
    qkv_part = inner_rows(gathered_one, qkv_back)
    normed_one_grad = lax.psum_scatter(
        outer_cols(qkv_back, qkv_full).astype(jnp.bfloat16),
        "tensor",
        scatter_dimension=0,
        tiled=True,
    ).astype(jnp.float32)
    norm_one_value, norm_one_pull = jax.vjp(layer_norm, tokens, vectors[0], vectors[1])
    token_part, gain_one, shift_one = norm_one_pull(normed_one_grad)
    input_grad = middle_grad + token_part
    vector_part = jnp.stack(
        [
            gain_one,
            shift_one,
            gain_two,
            shift_two,
            jnp.sum(middle_grad, axis=0),
            jnp.sum(cotangent, axis=0),
        ],
        axis=0,
    )
    bias_width = bias_part.shape[0]
    bias_offset = lax.axis_index("tensor") * bias_width
    bias_padded = lax.dynamic_update_slice_in_dim(
        jnp.zeros((FF,), jnp.float32), bias_part, bias_offset, 0
    )
    vector_total, bias_total = lax.psum((vector_part, bias_padded), ("dp", "tensor"))
    bias_total = lax.dynamic_slice_in_dim(bias_total, bias_offset, bias_width, 0)
    qkv_total, out_total, up_total, down_total = (
        lax.psum_scatter(
            qkv_part.astype(jnp.bfloat16), "dp", scatter_dimension=0, tiled=True
        ).astype(jnp.float32),
        lax.psum_scatter(
            out_part.astype(jnp.bfloat16), "dp", scatter_dimension=1, tiled=True
        ).astype(jnp.float32),
        lax.psum_scatter(
            up_part.astype(jnp.bfloat16), "dp", scatter_dimension=0, tiled=True
        ).astype(jnp.float32),
        lax.psum_scatter(
            down_part.astype(jnp.bfloat16), "dp", scatter_dimension=1, tiled=True
        ).astype(jnp.float32),
    )
    vec_res = adam_step(vectors, vector_total, vectors_m, vectors_v, 0.3, 0.0)
    qkv_res = adam_step(w_qkv, qkv_total, qkv_m, qkv_v, 0.1, 0.05)
    out_res = adam_step(w_out, out_total, out_m, out_v, 0.2, 0.05)
    up_res = adam_step(w_up, up_total, up_m, up_v, 0.1, 0.05)
    bias_res = adam_step(hidden_bias, bias_total, bias_m, bias_v, 0.3, 0.0)
    down_res = adam_step(w_down, down_total, down_m, down_v, 0.05, 0.05)
    return (
        output,
        input_grad,
        vec_res[0],
        vec_res[1],
        vec_res[2],
        vec_res[3],
        qkv_res[0],
        qkv_res[1],
        qkv_res[2],
        qkv_res[3],
        out_res[0],
        out_res[1],
        out_res[2],
        out_res[3],
        up_res[0],
        up_res[1],
        up_res[2],
        up_res[3],
        bias_res[0],
        bias_res[1],
        bias_res[2],
        bias_res[3],
        down_res[0],
        down_res[1],
        down_res[2],
        down_res[3],
    )


def solution(mesh):
    in_specs = (
        P(("dp", "tensor"), None),
        P(("dp", "tensor"), None),
        P(),
        P(),
        P(),
        P("dp", "tensor"),
        P("dp", "tensor"),
        P("dp", "tensor"),
        P("tensor", "dp"),
        P("tensor", "dp"),
        P("tensor", "dp"),
        P("dp", "tensor"),
        P("dp", "tensor"),
        P("dp", "tensor"),
        P("tensor"),
        P("tensor"),
        P("tensor"),
        P("tensor", "dp"),
        P("tensor", "dp"),
        P("tensor", "dp"),
    )
    out_specs = (
        P(("dp", "tensor"), None),
        P(("dp", "tensor"), None),
        P(),
        P(),
        P(),
        P(),
        P("dp", "tensor"),
        P("dp", "tensor"),
        P("dp", "tensor"),
        P("dp", "tensor"),
        P("tensor", "dp"),
        P("tensor", "dp"),
        P("tensor", "dp"),
        P("tensor", "dp"),
        P("dp", "tensor"),
        P("dp", "tensor"),
        P("dp", "tensor"),
        P("dp", "tensor"),
        P("tensor"),
        P("tensor"),
        P("tensor"),
        P("tensor"),
        P("tensor", "dp"),
        P("tensor", "dp"),
        P("tensor", "dp"),
        P("tensor", "dp"),
    )
    return jax.shard_map(
        per_device, mesh=mesh, in_specs=in_specs, out_specs=out_specs, check_vma=False
    )
```

profile of v0, /device:TPU:10, one launch (start us, length us, event | category | flops | bytes accessed | tf_op | source)
XLA Modules:
  0.0 935.0 jit_solution(4473717673103093042)
XLA Ops:
  7.3 1.8 reduce_sum.150
  10.8 1.3 add_convert_fusion.1
  12.2 10.7 %all_gather.29 = bf16[128,1024]{1,0:T(8,128)(2,1)} all-gather(bf16[128,256]{1,0:T(8,128)(2,1)S(1)} %convert_element_type.101), channel_id=1, replica_groups=mesh['dp'=4,'tensor'=8] {'dp'}, dimensions={1}, use_global_device_ids=true | all-gather | bytes 327680 | tf_op jit(solution)/shard_map/all_gather | solution.py:75
  22.9 10.9 %all_gather.28 = bf16[1024,384]{1,0:T(8,128)(2,1)S(1)} all-gather(bf16[256,384]{1,0:T(8,128)(2,1)S(1)} %convert_element_type.99), channel_id=1, replica_groups=mesh['dp'=4,'tensor'=8] {'dp'}, dimensions={0}, use_global_device_ids=true | all-gather | bytes 983040 | tf_op jit(solution)/shard_map/all_gather | solution.py:74
  33.9 48.4 %all-gather.8.cloned.1.call-done = bf16[3456,1024]{1,0:T(8,128)(2,1)} async-done(((bf16[432,1024]{1,0:T(8,128)(2,1)}), bf16[3456,1024]{1,0:T(8,128)(2,1)}) %all-gather.8.cloned.1.call-update) | async-done | bytes 7077904 | tf_op jit(solution)/shard_map/all_gather | solution.py:80
  82.2 8.4 convolution_convert_fusion.2
  90.7 12.3 %reshape.190 = bf16[6,576,2,3,64]{4,3,2,1,0:T(4,128)(2,1)} reshape(bf16[3456,384]{1,0:T(8,128)(2,1)} %convolution_convert_fusion.2) | data formatting | bytes 5308416 | tf_op jit(solution)/shard_map/reshape | solution.py:84
  103.0 10.0 %copy.71 = bf16[6,576,2,3,64]{1,4,2,3,0:T(8,128)(2,1)} copy(bf16[6,576,2,3,64]{4,3,2,1,0:T(4,128)(2,1)} %reshape.190) | data formatting | bytes 5308416 | tf_op jit(solution)/shard_map/while | solution.py:109
  112.9 26.4 %while.22 = (s32[]{:T(128)}, bf16[6,576,128]{2,1,0:T(8,128)(2,1)}, f32[6,2,576]{2,1,0:T(2,128)}, bf16[6,576,2,3,64]{1,4,2,3,0:T(8,128)(2,1)}, s32[]{:T(128)}) while((s32[]{:T(128)}, bf16[6,576,128]{2,1,0:T(8,128)(2,1)}, f32[6,2,576]{2,1,0:T(2,128)}, bf16[6,576,2,3,64]{1,4,2,3,0:T(8,128)(2,1)}, s32[]{:T(128)}) %tuple.81), condition=%wide.region_5.6_spmd, body=%wide.region_2.5_spmd.sunk | while | flops 175913856 | bytes 10409553 | solution.py:109
  112.9 1.1 dynamic-slice_bitcast_fusion.6
  117.4 1.1 dynamic-slice_bitcast_fusion.6
  121.8 1.1 dynamic-slice_bitcast_fusion.6
  126.1 1.1 dynamic-slice_bitcast_fusion.6
  130.5 1.1 dynamic-slice_bitcast_fusion.6
  134.9 1.1 dynamic-slice_bitcast_fusion.6
  139.3 6.3 all-to-all-start
  146.5 18.8 %all-to-all-done = bf16[8,432,128]{2,1,0:T(8,128)(2,1)S(1)} async-done(((bf16[8,432,128]{2,1,0:T(8,128)(2,1)}), bf16[8,432,128]{2,1,0:T(8,128)(2,1)S(1)}, u32[]{:S(2)}, u32[]{:S(2)}) %all-to-all-start) | async-done | bytes 884768 | tf_op jit(solution)/shard_map/all_to_all | solution.py:111
  166.2 3.1 fusion.63
  169.6 1.3 add_convert_fusion
  170.9 1.8 convert_element_type.105
  172.8 1.7 fusion.61
  175.0 1.4 all-gather.14.cloned.1.call-done
  176.4 71.0 %all-gather.12.cloned.1.call-done = bf16[3456,1024]{1,0:T(8,128)(2,1)} async-done(((bf16[432,1024]{1,0:T(8,128)(2,1)}), bf16[3456,1024]{1,0:T(8,128)(2,1)}) %all-gather.12.cloned.1.call-update) | async-done | bytes 7077904 | tf_op jit(solution)/shard_map/all_gather | solution.py:116
  247.4 10.0 %convolution_add_fusion = f32[3456,512]{1,0:T(8,128)} fusion(bf16[3456,1024]{1,0:T(8,128)(2,1)} %all-gather.12.cloned.1.call-done, bf16[1024,512]{1,0:T(8,128)(2,1)} %all-gather.14.cloned.1.call-done, f32[512]{0:T(512)} %param.38), kind=kOutput, calls=%fused_computation.59 | convolution fusion | flops 3625648128 | bytes 15206400 | tf_op jit(solution)/shard_map/dot_general | solution.py:21
  257.5 19.7 %all-gather.16.cloned.1.call-done = bf16[512,1024]{1,0:T(8,128)(2,1)} async-done(((bf16[512,256]{1,0:T(8,128)(2,1)}), bf16[512,1024]{1,0:T(8,128)(2,1)}) %all-gather.16.cloned.1.call-update) | async-done | bytes 1048592 | tf_op jit(solution)/shard_map/all_gather | solution.py:77
  277.1 71.0 %all-gather.18.cloned.1.call-done = bf16[3456,1024]{1,0:T(8,128)(2,1)} async-done(((bf16[432,1024]{1,0:T(8,128)(2,1)}), bf16[3456,1024]{1,0:T(8,128)(2,1)}) %all-gather.18.cloned.1.call-update) | async-done | bytes 7077904 | tf_op jit(solution)/shard_map/all_gather | solution.py:126
  348.1 23.9 %fusion.57 = (f32[512]{0:T(512)}, bf16[3456,512]{1,0:T(8,128)(2,1)S(1)}, f32[3456,512]{1,0:T(8,128)}) fusion(f32[3456,512]{1,0:T(8,128)} %convolution_add_fusion, bf16[3456,1024]{1,0:T(8,128)(2,1)} %all-gather.18.cloned.1.call-done, bf16[512,1024]{1,0:T(8,128)(2,1)} %all-gather.16.cloned.1.call-done), kind=kOutput, calls=%fused_computation.126 | convolution fusion | flops 3753049600 | bytes 25823232 | tf_op jit(solution)/shard_map/dot_general | solution.py:31
  372.1 1.7 copy-done.32
  373.8 7.3 fusion.35
  381.4 7.0 multiply_convert_fusion.1
  388.4 1.8 copy-done.6
  390.2 5.8 convolution_convert_fusion
  396.0 127.5 %reduce-scatter.10.cloned.1.call-done = f32[432,1024]{1,0:T(8,128)} async-done(((f32[3456,1024]{1,0:T(8,128)}), f32[432,1024]{1,0:T(8,128)}) %reduce-scatter.10.cloned.1.call-update) | async-done | bytes 1769488 | tf_op jit(solution)/shard_map/reduce_scatter | solution.py:134
  523.5 2.8 multiply_reduce_fusion.2
  527.0 74.5 %reduce-scatter.8.cloned.1.call-done = bf16[432,1024]{1,0:T(8,128)(2,1)} async-done(((bf16[3456,1024]{1,0:T(8,128)(2,1)}), bf16[432,1024]{1,0:T(8,128)(2,1)}) %reduce-scatter.8.cloned.1.call-update) | async-done | bytes 884752 | tf_op jit(solution)/shard_map/reduce_scatter | solution.py:119
  601.5 3.2 fusion.60
  605.6 1.1 convert_element_type.110
  606.7 9.1 fusion.37
  615.9 9.7 %convolution_convert_fusion.4 = bf16[512,1024]{1,0:T(8,128)(2,1)} fusion(bf16[3456,512]{1,0:T(8,128)(2,1)} %copy-done.6, bf16[3456,1024]{1,0:T(8,128)(2,1)} %all-gather.18.cloned.1.call-done), kind=kOutput, calls=%fused_computation.85 | convolution fusion | flops 3624402944 | bytes 11665408 | tf_op jit(solution)/shard_map/dot_general | solution.py:25
  625.9 50.9 %all-gather.20.cloned.1.call-done = bf16[3456,1024]{1,0:T(8,128)(2,1)} async-done(((bf16[432,1024]{1,0:T(8,128)(2,1)}), bf16[3456,1024]{1,0:T(8,128)(2,1)}) %all-gather.20.cloned.1.call-update) | async-done | bytes 7077904 | tf_op jit(solution)/shard_map/all_gather | solution.py:140
  676.8 5.9 convolution_convert_fusion.3
  682.8 46.1 %while.23 = (s32[]{:T(128)}, bf16[6,576,384]{2,1,0:T(8,128)(2,1)}, bf16[6,576,2,3,64]{1,4,2,3,0:T(8,128)(2,1)}, f32[6,2,576]{2,1,0:T(2,128)}, bf16[6,576,128]{2,1,0:T(8,128)(2,1)}, /*index=5*/s32[]{:T(128)}) while((s32[]{:T(128)}, bf16[6,576,384]{2,1,0:T(8,128)(2,1)}, bf16[6,576,2,3,64]{1,4,2,3,0:T(8,128)(2,1)}, f32[6,2,576]{2,1,0:T(2,128)}, ...), condition=%wide.region_14.15_spmd, body=%wide.region_12.14_spmd.sunk | while | flops 433445760 | bytes 27115612 | solution.py:177
  684.6 1.1 dynamic-slice_bitcast_fusion.7
  692.2 1.1 dynamic-slice_bitcast_fusion.7
  699.9 1.1 dynamic-slice_bitcast_fusion.7
  707.6 1.1 dynamic-slice_bitcast_fusion.7
  715.3 1.1 dynamic-slice_bitcast_fusion.7
  723.0 1.1 dynamic-slice_bitcast_fusion.7
  728.9 5.1 convolution_convert_fusion.6
  734.1 8.6 convolution_convert_fusion.5
  743.1 7.7 convolution_convert_fusion.1
  752.1 2.6 multiply_subtract_fusion.1
  754.6 2.7 multiply_subtract_fusion
  757.4 9.7 %reduce-scatter.16.cloned.1.call-done = bf16[128,256]{1,0:T(8,128)(2,1)} async-done(((bf16[128,1024]{1,0:T(8,128)(2,1)}), bf16[128,256]{1,0:T(8,128)(2,1)}) %reduce-scatter.16.cloned.1.call-update) | async-done | bytes 65552 | tf_op jit(solution)/shard_map/reduce_scatter | solution.py:213
  767.1 1.8 multiply_subtract_fusion.3
  768.9 27.5 %reduce-scatter.14.cloned.1.call-done = bf16[256,384]{1,0:T(8,128)(2,1)} async-done(((bf16[1024,384]{1,0:T(8,128)(2,1)}), bf16[256,384]{1,0:T(8,128)(2,1)}) %reduce-scatter.14.cloned.1.call-update) | async-done | bytes 196624 | tf_op jit(solution)/shard_map/reduce_scatter | solution.py:210
  796.4 2.5 multiply_subtract_fusion.2
  798.9 74.3 %reduce-scatter.12.cloned.1.call-done = bf16[432,1024]{1,0:T(8,128)(2,1)} async-done(((bf16[3456,1024]{1,0:T(8,128)(2,1)}), bf16[432,1024]{1,0:T(8,128)(2,1)}) %reduce-scatter.12.cloned.1.call-update) | async-done | bytes 884752 | tf_op jit(solution)/shard_map/reduce_scatter | solution.py:182
  873.2 2.4 convert_reduce_fusion
  877.2 1.4 stack.31
  878.6 43.6 %all-reduce = (f32[6,1024]{1,0:T(8,128)}, f32[4096]{0:T(1024)}) all-reduce(f32[6,1024]{1,0:T(8,128)} %stack.31, f32[4096]{0:T(1024)} %copy-done.22), channel_id=1, replica_groups=mesh['dp'=4,'tensor'=8] {'dp','tensor'}, use_global_device_ids=true, to_apply=%region_24.25 | all-reduce | flops 10240 | bytes 81920 | tf_op jit(solution)/shard_map/psum | solution.py:207
  922.2 1.4 multiply_subtract_fusion.5
  923.6 1.5 multiply_subtract_fusion.4
  925.1 3.0 add_add_fusion.2
  (230 shorter events, 69.0 us)
Async XLA Ops:
  7.2 2.0 copy-start
  7.2 2.3 copy-start.19
  7.2 75.0 %all-gather.8.cloned.1.call-start = ((), (), s32[]{:S(2)}) async-start(), calls=%async_computation.8 | async-start | bytes 7962624 | tf_op jit(solution)/shard_map/all_gather | solution.py:80
  9.0 3.1 copy-start.16
  9.2 1.0 copy-start.20
  9.2 13.7 %copy-start.10 = (f32[256,384]{1,0:T(8,128)S(1)}, f32[256,384]{1,0:T(8,128)}, u32[]{:S(2)}) copy-start(f32[256,384]{1,0:T(8,128)} %param.29) | copy-start | bytes 1179652
  9.5 0.7 copy-start.25
  9.6 13.3 %copy-start.23 = (f32[432]{0:T(512)}, f32[432]{0:T(512)S(1)}, u32[]{:S(2)}) copy-start(f32[432]{0:T(512)S(1)} %fusion.48) | copy-start | bytes 5188
  10.2 0.6 copy-start.17
  12.1 134.4 %all-gather.10.cloned.1.call-start = ((), (), s32[]{:S(2)}) async-start(), calls=%async_computation.9 | async-start | bytes 2359296 | tf_op jit(solution)/shard_map/all_gather | solution.py:112
  33.9 56.8 %copy-start.13 = (bf16[1024,384]{1,0:T(8,128)(2,1)}, bf16[1024,384]{1,0:T(8,128)(2,1)S(1)}, u32[]{:S(2)}) copy-start(bf16[1024,384]{1,0:T(8,128)(2,1)S(1)} %all_gather.28) | copy-start | bytes 2359300
  112.9 32.7 %copy-start.7 = (f32[256,512]{1,0:T(8,128)S(1)}, f32[256,512]{1,0:T(8,128)}, u32[]{:S(2)}) copy-start(f32[256,512]{1,0:T(8,128)} %param.35) | copy-start | bytes 1572868
  139.3 25.9 %all-to-all-start = ((bf16[8,432,128]{2,1,0:T(8,128)(2,1)}), bf16[8,432,128]{2,1,0:T(8,128)(2,1)S(1)}, u32[]{:S(2)}, u32[]{:S(2)}) async-start(bf16[8,432,128]{2,1,0:T(8,128)(2,1)} %bitcast.22), calls=%async_computation | async-start | bytes 1769472 | tf_op jit(solution)/shard_map/all_to_all | solution.py:111
  145.6 30.8 %all-gather.14.cloned.1.call-start = ((), (), s32[]{:S(2)}) async-start(), calls=%async_computation.11 | async-start | bytes 1310720 | tf_op jit(solution)/shard_map/all_gather | solution.py:76
  146.4 101.0 %all-gather.12.cloned.1.call-start = ((), (), s32[]{:S(2)}) async-start(), calls=%async_computation.10 | async-start | bytes 7962624 | tf_op jit(solution)/shard_map/all_gather | solution.py:116
  165.2 0.9 copy-start.12
  166.2 3.4 copy-start.28
  169.2 3.5 copy-start.3
  170.9 106.3 %all-gather.16.cloned.1.call-start = ((), (), s32[]{:S(2)}) async-start(), calls=%async_computation.12 | async-start | bytes 1310720 | tf_op jit(solution)/shard_map/all_gather | solution.py:77
  172.7 175.4 %all-gather.18.cloned.1.call-start = ((), (), s32[]{:S(2)}) async-start(), calls=%async_computation.14 | async-start | bytes 7962624 | tf_op jit(solution)/shard_map/all_gather | solution.py:126
  174.5 349.1 %reduce-scatter.10.cloned.1.call-start = ((), (), s32[]{:S(2)}) async-start(), calls=%async_computation.15 | async-start | bytes 15925248 | tf_op jit(solution)/shard_map/reduce_scatter | solution.py:134
  257.5 116.4 %copy-start.30 = (bf16[1024,512]{1,0:T(8,128)(2,1)S(1)}, bf16[1024,512]{1,0:T(8,128)(2,1)}, u32[]{:S(2)}) copy-start(bf16[1024,512]{1,0:T(8,128)(2,1)} %all-gather.14.cloned.1.call-done) | copy-start | bytes 3145732
  372.1 1.7 copy-start.32
  381.1 220.3 %reduce-scatter.8.cloned.1.call-start = ((), (), s32[]{:S(2)}) async-start(), calls=%async_computation.13 | async-start | bytes 7962624 | tf_op jit(solution)/shard_map/reduce_scatter | solution.py:119
  381.4 8.8 copy-start.31
  388.4 1.8 copy-start.6
  396.0 280.9 %all-gather.20.cloned.1.call-start = ((), (), s32[]{:S(2)}) async-start(), calls=%async_computation.16 | async-start | bytes 7962624 | tf_op jit(solution)/shard_map/all_gather | solution.py:140
  523.5 77.9 %copy-start.5 = (f32[432,1024]{1,0:T(8,128)S(1)}, f32[432,1024]{1,0:T(8,128)}, u32[]{:S(2)}) copy-start(f32[432,1024]{1,0:T(8,128)} %reduce-scatter.10.cloned.1.call-done) | copy-start | bytes 5308420
  601.5 3.3 copy-start.4
  606.7 145.0 %reduce-scatter.18.cloned.1.call-start = ((), (), s32[]{:S(2)}) async-start(), calls=%async_computation.20 | async-start | bytes 1310720 | tf_op jit(solution)/shard_map/reduce_scatter | solution.py:216
  615.8 138.8 %reduce-scatter.20.cloned.1.call-start = ((), (), s32[]{:S(2)}) async-start(), calls=%async_computation.21 | async-start | bytes 1310720 | tf_op jit(solution)/shard_map/reduce_scatter | solution.py:219
  615.9 61.0 %copy-start.11 = (bf16[128,1024]{1,0:T(8,128)(2,1)S(1)}, bf16[128,1024]{1,0:T(8,128)(2,1)}, u32[]{:S(2)}) copy-start(bf16[128,1024]{1,0:T(8,128)(2,1)} %all_gather.29) | copy-start | bytes 786436
  625.6 141.4 %reduce-scatter.16.cloned.1.call-start = ((), (), s32[]{:S(2)}) async-start(), calls=%async_computation.19 | async-start | bytes 327680 | tf_op jit(solution)/shard_map/reduce_scatter | solution.py:213
  734.1 62.3 %reduce-scatter.14.cloned.1.call-start = ((), (), s32[]{:S(2)}) async-start(), calls=%async_computation.18 | async-start | bytes 983040 | tf_op jit(solution)/shard_map/reduce_scatter | solution.py:210
  734.1 9.0 copy-start.14
  742.8 130.4 %reduce-scatter.12.cloned.1.call-start = ((), (), s32[]{:S(2)}) async-start(), calls=%async_computation.17 | async-start | bytes 7962624 | tf_op jit(solution)/shard_map/reduce_scatter | solution.py:182
  750.8 0.7 copy-start.29
  750.8 1.1 copy-start.8
  750.8 1.2 copy-start.15
  750.9 3.8 copy-start.9
  751.7 2.9 copy-start.22
  757.3 115.8 %copy-start.1 = (f32[432,1024]{1,0:T(8,128)S(1)}, f32[432,1024]{1,0:T(8,128)}, u32[]{:S(2)}) copy-start(f32[432,1024]{1,0:T(8,128)} %param.24) | copy-start | bytes 5308420
  757.3 115.8 %copy-start.18 = (f32[1,1024]{1,0:T(1,128)S(1)}, f32[1,1024]{1,0:T(1,128)}, u32[]{:S(2)}) copy-start(f32[1,1024]{1,0:T(1,128)} %copy-done.17) | copy-start | bytes 12292
  757.3 115.8 %copy-start.21 = (f32[432]{0:T(512)S(1)}, f32[432]{0:T(512)}, u32[]{:S(2)}) copy-start(f32[432]{0:T(512)} %copy-done.20) | copy-start | bytes 5188
  768.9 106.7 %copy-start.26 = (f32[432]{0:T(512)S(1)}, f32[432]{0:T(512)}, u32[]{:S(2)}) copy-start(f32[432]{0:T(512)} %copy-done.25) | copy-start | bytes 5188
  768.9 106.7 %copy-start.24 = (f32[432]{0:T(512)S(1)}, f32[432]{0:T(512)}, u32[]{:S(2)}) copy-start(f32[432]{0:T(512)} %copy-done.23) | copy-start | bytes 5188
  873.2 2.4 copy-start.2
  875.6 1.0 copy-start.27
Sparse Core Ops, SparseCore 0:
  12.2 70.0 all-gather.7
  83.8 30.0 all-gather.9
  148.9 27.4 all-gather.13
  178.5 68.8 all-gather.11
  249.7 27.4 all-gather.15
  279.2 68.9 all-gather.17
  381.2 142.2 reduce-scatter.9
  525.8 75.5 reduce-scatter.7
  606.8 70.0 all-gather.19
  680.1 28.6 reduce-scatter.17
  712.0 27.7 reduce-scatter.19
  743.0 24.0 reduce-scatter.15
  770.2 26.1 reduce-scatter.13
  798.6 74.4 reduce-scatter.11
where the time goes:
time: 944 us; the launch traced here: 935 us
  waiting for transfers between devices  595 us (63%)
  matrix products  131 us (14%)
  local copies, waits for them, and re-layouts  65.9 us (7%)
  blocking collectives  65.3 us (7%)
  other arithmetic  55.3 us (6%)
  between operations  14.7 us (2%)
    reduce_scatter x1, waiting for transfers between devices, per_device(): lax.psum_scatter(outer_cols(pre_low, up_full), 'tensor', scatter_dimensio...  127 us
    reduce_scatter x1, waiting for transfers between devices, per_device(): lax.psum_scatter(matmul(hidden_low, down_full).astype(jnp.bfloat16), 'ten...  74.5 us
    reduce_scatter x1, waiting for transfers between devices, per_device(): lax.psum_scatter(outer_cols(qkv_back, qkv_full).astype(jnp.bfloat16), 'te...  74.3 us
    all_gather x1, waiting for transfers between devices, per_device(): lax.all_gather(cotangent.astype(jnp.bfloat16), 'tensor', axis=0, tiled=True)  71 us
    all_gather x1, waiting for transfers between devices, per_device(): lax.all_gather(normed_two.astype(jnp.bfloat16), 'tensor', axis=0, tiled=T...  71 us
    all_gather x1, waiting for transfers between devices, per_device(): lax.all_gather(middle_grad.astype(jnp.bfloat16), 'tensor', axis=0, tiled=...  50.9 us
    all_gather x1, waiting for transfers between devices, per_device(): lax.all_gather(normed_one.astype(jnp.bfloat16), 'tensor', axis=0, tiled=T...  48.4 us
    dot_general x4, matrix products, outer_cols(): lax.dot_general(left, right, (((1,), (1,)), ((), ())), preferred_element_...  44.9 us
  transfers between devices with their start and end apart: 15, of which 12 were waited for; matrix products, arithmetic and copies ran while one was open for 21% of the time, Pallas kernels for 0%

commit v1 on v0

v1 whole, which is shorter than its diff:
```python
import math

import jax
import jax.numpy as jnp
from jax import lax
from jax.experimental import pallas as pl
from jax.experimental.pallas import tpu as pltpu
from jax.sharding import PartitionSpec as P

HD = 64
SEQ = 576
STEP = 10
NZ = 4
BIAS_ROWS = 16
AXES = ("dp", "tensor")
F32 = jnp.float32
BF16 = jnp.bfloat16
VMEM_LIMIT = 63 * 1024 * 1024
TIMES = {"first_norm": 5, "attend_whole_back": 1000}


def nn(left, right):
    return jnp.dot(left, right, preferred_element_type=F32)


def nt(left, right):
    return lax.dot_general(left, right, (((1,), (1,)), ((), ())), preferred_element_type=F32)


def tn(left, right):
    return lax.dot_general(left, right, (((0,), (0,)), ((), ())), preferred_element_type=F32)


def cost(name, nbytes):
    return pl.CostEstimate(flops=int(5e8 * TIMES.get(name, 0)), bytes_accessed=int(nbytes), transcendentals=0)


def call(body, name, grid, scalars, in_specs, out_specs, out_shape, args, scratch=(), after=(), hold=(), nbytes=0):
    given, extra = len(args), len(after) + len(hold)
    single = not isinstance(out_shape, (list, tuple))
    out_specs, out_shape = ([out_specs], [out_shape]) if single else (list(out_specs), list(out_shape))
    made = len(out_shape)

    def run(sc, *refs):
        rest = refs[given + extra :]
        body(sc, *refs[:given], *rest[:made], *rest[made + len(hold) :])

    anywhere = pl.BlockSpec(memory_space=pltpu.HBM)
    first = 1 + given + len(after)
    out = pl.pallas_call(
        run,
        name=name,
        grid_spec=pltpu.PrefetchScalarGridSpec(
            num_scalar_prefetch=1,
            grid=grid,
            in_specs=list(in_specs) + [anywhere] * extra,
            out_specs=out_specs + [anywhere] * len(hold),
            scratch_shapes=list(scratch),
        ),
        out_shape=out_shape + [shape(h.shape, h.dtype) for h in hold],
        input_output_aliases={first + i: made + i for i in range(len(hold))},
        compiler_params=pltpu.CompilerParams(vmem_limit_bytes=VMEM_LIMIT),
        cost_estimate=cost(name, nbytes),
    )(scalars, *args, *after, *hold)
    return out[0] if single and not hold else tuple(out)


def shape(dims, dtype):
    return jax.ShapeDtypeStruct(dims, dtype)


def whole(dims):
    return pl.BlockSpec(dims, lambda *_: (0,) * len(dims))


def slot(dims):
    return pl.BlockSpec((1,) + dims, lambda s, *_: (s, 0, 0))


def lower_slots(dims):
    return pl.BlockSpec((1,) + dims, lambda s, *_: (jnp.minimum(s, NZ // 2 - 1), 0, 0))


def upper_slots(dims):
    return pl.BlockSpec((1,) + dims, lambda s, *_: (jnp.maximum(s - NZ // 2, 0), 0, 0))


class Copies:
    def __init__(self, sems):
        self.sems, self.used = sems, 0

    def start(self, source, target):
        copy = pltpu.make_async_copy(source, target, self.sems.at[self.used])
        self.used += 1
        copy.start()
        return copy


def wait(copies):
    for copy in copies:
        copy.wait()


def manual(body, name, scalars, args, out_shape, scratch, copies, after=(), hold=()):
    given, extra = len(args), len(after) + len(hold)
    nbytes = sum(math.prod(a.shape) * a.dtype.itemsize for a in list(args) + list(out_shape))

    def run(sc, *refs):
        rest = refs[given + extra :]
        body(sc, refs[:given], rest[: len(out_shape)], rest[len(out_shape) + len(hold) : -1], Copies(rest[-1]))

    anywhere = pl.BlockSpec(memory_space=pltpu.HBM)
    first = 1 + given + len(after)
    return pl.pallas_call(
        run,
        name=name,
        in_specs=[pl.BlockSpec(memory_space=pltpu.SMEM)] + [anywhere] * (given + extra),
        out_specs=[anywhere] * (len(out_shape) + len(hold)),
        out_shape=list(out_shape) + [shape(h.shape, h.dtype) for h in hold],
        input_output_aliases={first + i: len(out_shape) + i for i in range(len(hold))},
        scratch_shapes=list(scratch) + [pltpu.SemaphoreType.DMA((copies,))],
        compiler_params=pltpu.CompilerParams(vmem_limit_bytes=VMEM_LIMIT),
        cost_estimate=cost(name, nbytes),
    )(scalars, *args, *after, *hold)


def vmem(dims, dtype=BF16):
    return pltpu.VMEM(dims, dtype)


class Weights:
    def __init__(self, arrays, blocks, block, col, cols):
        full = arrays[0].shape[2]
        if (col % 128 or cols % 128) and cols != full:
            arrays, col, full = [a[:, :, col : col + cols] for a in arrays], 0, cols
        self.args, self.blocks, self.block = list(arrays), blocks, block
        self.col, self.cols, self.full = col, cols, full
        self.depth = block * len(blocks)
        self.flat = cols % 128 == 0
        self.scratch = vmem((self.depth, NZ * cols) if self.flat else (NZ, self.depth, cols))
        self.copies = len(blocks) * NZ

    def load(self, copies, refs, target, sc):
        by_slot = [[] for _ in range(NZ)]
        for z in range(NZ):
            for k, (row, places) in enumerate(self.blocks):
                number, place = places[z]
                source = refs[number].at[sc[3] ^ z if place is None else place, pl.ds(row, self.block), :]
                if self.cols != self.full:
                    source = source.at[:, pl.ds(self.col, self.cols)]
                rows = pl.ds(k * self.block, self.block)
                goal = target.at[rows, pl.ds(z * self.cols, self.cols)] if self.flat else target.at[z, rows, :]
                by_slot[z].append(copies.start(source, goal))
        return by_slot

    def slots(self, target, first, count):
        if self.flat:
            return target[:, first * self.cols : (first + count) * self.cols]
        assert count == 1
        return target[first]


def slots_at_once(cols):
    for step in (1, 2, 4):
        if cols * step % 512 == 0 and cols % 128 == 0:
            return step
    return 1


class Rows:
    def __init__(self, parts, ordered, swapped=0):
        self.ordered, self.swapped = ordered, swapped
        self.part = parts[0].shape[0]
        self.args = list(parts)
        self.count = self.part * len(parts)
        self.width = parts[0].shape[1]
        self.copies = len(parts) * max(1, swapped)

    def load(self, copies, refs, target, sc, first=0):
        started = []
        for j, ref in enumerate(refs):
            at = first + j * self.part
            if self.ordered and len(refs) > 1:
                at = pl.multiple_of((sc[1] ^ j) * self.part, 16)
            rows = pl.ds(at, self.part)
            if not self.swapped:
                started.append(copies.start(ref, target.at[rows, :]))
                continue
            block = self.width // self.swapped
            for k in range(self.swapped):
                source = ref.at[:, pl.ds((k ^ 1) * block, block)]
                started.append(copies.start(source, target.at[rows, pl.ds(k * block, block)]))
        return started


class Slots:
    def __init__(self, array):
        self.args, self.copies = [array], NZ
        _, self.count, self.cols = array.shape

    def load(self, copies, refs, target, sc, first=0):
        return [[copies.start(refs[0].at[z], target.at[z, pl.ds(first, self.count), :])] for z in range(NZ)]


class SplitSlots:
    def __init__(self, full, mine, theirs):
        self.args, self.copies = [full, mine, theirs], 2 * NZ
        self.count, self.cols = full.shape[1] + mine.shape[1], full.shape[2]

    def load(self, copies, refs, target, sc, first=0):
        full, mine, theirs = refs
        by_slot = [[copies.start(full.at[z], target.at[z, whole_image(sc), :])] for z in range(NZ)]
        for z in range(NZ):
            source = (theirs if z % 2 else mine).at[z // 2]
            by_slot[z].append(copies.start(source, target.at[z, split_rows(sc), :]))
        return by_slot


def take(items, count):
    return items[:count], items[count:]


def store_parts(total, out_scratch, parts, copies, outs, sc, ordered, swapped):
    part = out_scratch.shape[1]
    started = []
    for j in range(parts):
        rows = pl.ds(pl.multiple_of((sc[1] ^ j) * part, 8) if ordered else j * part, part)
        if swapped:
            block = total.shape[1] // swapped
            for k in range(swapped):
                piece = total[rows, k * block : (k + 1) * block]
                out_scratch[j, :, (k ^ 1) * block : ((k ^ 1) + 1) * block] = piece.astype(BF16)
        else:
            out_scratch[j] = total[rows, :].astype(BF16)
        started.append(copies.start(out_scratch.at[j], outs[j]))
    return started


def gate(scalars, after, hold):
    def body(sc, ins, outs, scratch, copies):
        pass

    return manual(body, "gate", scalars, [], [], [], 1, after, hold)


def pack(scalars, pieces, after=(), hold=()):
    def body(sc, ins, outs, scratch, copies):
        arriving = [copies.start(ref, scratch[0].at[i]) for i, ref in enumerate(ins)]
        leaving = []
        for i, copy in enumerate(arriving):
            copy.wait()
            leaving.append(copies.start(scratch[0].at[i], outs[0].at[i]))
        wait(leaving)

    dims = (len(pieces),) + pieces[0].shape
    return manual(
        body, "pack", scalars, pieces, [shape(dims, BF16)], [vmem(dims)], 2 * len(pieces), after, hold
    )


def add(scalars, arrays, after=(), hold=()):
    out, *held = add_groups(scalars, [arrays], False, after, hold)
    return (out, *held)


def add_groups(scalars, groups, apart, after=(), hold=()):
    dims, terms = groups[0][0].shape, len(groups[0])
    three = len(dims) == 3
    count = dims[0] if three else 3 if dims[0] % 48 == 0 else 1
    rows = 0 if three else dims[0] // count
    place = (lambda ref, i: ref.at[i]) if three else (lambda ref, i: ref.at[pl.ds(i * rows, rows), :])
    at = (lambda i: i) if three else (lambda i: slice(i * rows, (i + 1) * rows))

    def body(sc, ins, outs, scratch, copies):
        arriving = []
        for g in range(len(groups)):
            for i in range(count):
                arriving.append([
                    copies.start(place(ins[g * terms + t], i), place(scratch[g * terms + t], i)) for t in range(terms)
                ])
        leaving = []
        for g in range(len(groups)):
            total_ref = scratch[len(groups) * terms + g]
            for i in range(count):
                wait(arriving[g * count + i])
                total = scratch[g * terms][at(i)].astype(F32)
                for t in range(1, terms):
                    total += scratch[g * terms + t][at(i)].astype(F32)
                total_ref[at(i)] = total.astype(BF16)
                goal = outs[g * count + i] if apart else place(outs[g], i)
                leaving.append(copies.start(place(total_ref, i), goal))
        wait(leaving)

    made = [shape(dims[1:], BF16)] * (count * len(groups)) if apart else [shape(dims, BF16)] * len(groups)
    return manual(
        body, "add", scalars, [a for g in groups for a in g], made, [vmem(dims)] * ((terms + 1) * len(groups)),
        (terms + 1) * count * len(groups), after, hold,
    )


def project(scalars, rows, weights, name, after=(), hold=()):
    count, cols = rows.count, weights.cols
    half = SEQ // 2

    def body(sc, ins, outs, scratch, copies):
        x, w, y = scratch
        row_refs, weight_refs = take(ins, len(rows.args))
        started = rows.load(copies, row_refs, x, sc)
        by_slot = weights.load(copies, weight_refs, w, sc)
        wait(started)
        step, leaving = slots_at_once(cols), []
        for z in range(0, NZ, step):
            for s in range(z, z + step):
                wait(by_slot[s])
            value = nn(x[...], weights.slots(w, z, step))
            for s in range(step):
                y[z + s] = value[:, s * cols : (s + 1) * cols].astype(BF16)
                leaving.append(copies.start(y.at[z + s], outs[0].at[z + s]))
                if (z + s) % 2:
                    leaving.append(copies.start(y.at[z + s, split_rows(sc), :], outs[1].at[(z + s) // 2]))
        wait(leaving)

    return manual(
        body, name, scalars, rows.args + weights.args,
        [shape((NZ, count, cols), BF16), shape((NZ // 2, half, cols), BF16)],
        [vmem((count, rows.width)), weights.scratch, vmem((NZ, count, cols))],
        rows.copies + weights.copies + NZ + NZ // 2, after, hold,
    )


def project_back(scalars, slots, weights, nodes, name, after=(), hold=()):
    count, cols, width = slots.count, weights.cols, weights.depth

    def body(sc, ins, outs, scratch, copies):
        y, w, total, parts = scratch
        slot_refs, weight_refs = take(ins, len(slots.args))
        for started in slots.load(copies, slot_refs, y, sc) + weights.load(copies, weight_refs, w, sc):
            wait(started)
        if weights.flat:
            total[...] = nt(jnp.concatenate([y[z] for z in range(NZ)], axis=1), w[...])
        else:
            value = nt(y[0], w[0])
            for z in range(1, NZ):
                value += nt(y[z], w[z])
            total[...] = value
        wait(store_parts(total, parts, nodes, copies, outs, sc, True, 0))

    return manual(
        body, name, scalars, slots.args + weights.args, [shape((count // nodes, width), BF16)] * nodes,
        [vmem((NZ, count, cols)), weights.scratch, vmem((count, width), F32), vmem((nodes, count // nodes, width))],
        slots.copies + weights.copies + nodes, after, hold,
    )


def weight_grads(scalars, products, dps, out_shape, goal, side, name, after=(), hold=()):
    counts = [sum(g.count for g in rows) for rows, _ in products]
    widths = [slots[0].cols for _, slots in products]
    width = products[0][0][0].width
    block = width // dps
    parts = 1 if side else len(products)
    cols = sum(widths) if side else widths[0]
    step = max(slots_at_once(c) for c in widths)
    args, scratch, copies_needed = [], [vmem((parts, NZ, width, cols))], parts * NZ * dps
    for (rows, slots), count, own in zip(products, counts, widths):
        args += [a for g in rows + slots for a in g.args]
        scratch += [vmem((count, width)), vmem((NZ, count, own)), vmem((width, count))]
        copies_needed += sum(g.copies for g in rows + slots)

    def body(sc, ins, outs, scratch, copies):
        result = scratch[0]
        loaded = []
        for i, (rows, slots) in enumerate(products):
            x, y, flipped = scratch[1 + 3 * i : 4 + 3 * i]
            started, at = [], 0
            for g in rows:
                refs, ins = take(ins, len(g.args))
                started += g.load(copies, refs, x, sc, at)
                at += g.count
            by_slot, at = [[] for _ in range(NZ)], 0
            for g in slots:
                refs, ins = take(ins, len(g.args))
                for z, some in enumerate(g.load(copies, refs, y, sc, at)):
                    by_slot[z] += some
                at += g.count
            loaded.append((started, by_slot))
        leaving = []

        def send(part, z):
            for k in range(dps):
                rows = pl.ds(k * block, block)
                leaving.append(copies.start(result.at[part, z, rows, :], goal(sc, outs, part, k, z)))

        def multiply(i, z, at, part):
            y, flipped, own = scratch[2 + 3 * i], scratch[3 + 3 * i], widths[i]
            for s in range(z, z + step):
                wait(loaded[i][1][s])
            whole_y = jnp.concatenate([y[z + s] for s in range(step)], axis=1) if step > 1 else y[z]
            value = nn(flipped[...], whole_y)
            for s in range(step):
                result[part, z + s, :, at : at + own] = value[:, s * own : (s + 1) * own].astype(BF16)

        def flip(i):
            wait(loaded[i][0])
            scratch[3 + 3 * i][...] = scratch[1 + 3 * i][...].T

        if side:
            for i in range(len(products)):
                flip(i)
            for z in range(0, NZ, step):
                for i in range(len(products)):
                    multiply(i, z, sum(widths[:i]), 0)
                for s in range(z, z + step):
                    send(0, s)
        else:
            for i in range(len(products)):
                flip(i)
                for z in range(0, NZ, step):
                    multiply(i, z, 0, i)
                    for s in range(z, z + step):
                        send(i, s)
        wait(leaving)

    return list(manual(body, name, scalars, args, out_shape, scratch, copies_needed, after, hold))


def feed_forward(scalars, rows, weights, bias_row, name, after=(), hold=()):
    count, cols = rows.count, weights.cols

    def body(sc, ins, outs, scratch, copies):
        x, w, b, hidden, slope = scratch
        row_refs, weight_refs = take(ins, len(rows.args))
        started = rows.load(copies, row_refs, x, sc)
        for z in range(NZ):
            started.append(copies.start(weight_refs[0].at[sc[3] ^ z, pl.ds(bias_row, BIAS_ROWS), :], b.at[z]))
        by_slot = weights.load(copies, weight_refs, w, sc)
        wait(started)
        leaving = []
        step = slots_at_once(cols)
        for z in range(0, NZ, step):
            for s in range(z, z + step):
                wait(by_slot[s])
            value = nn(x[...], weights.slots(w, z, step))
            for s in range(step):
                terms = b[z + s].astype(F32)
                u = value[:, s * cols : (s + 1) * cols] + (terms[0:1] + terms[1:2] + terms[2:3])
                cdf = 0.5 + 0.5 * lax.erf(u * math.sqrt(0.5))
                hidden[z + s] = (u * cdf).astype(BF16)
                slope[z + s] = (cdf + u * (jnp.exp(-0.5 * u * u) * (1.0 / math.sqrt(2.0 * math.pi)))).astype(BF16)
                leaving.append(copies.start(hidden.at[z + s], outs[0].at[z + s]))
                leaving.append(copies.start(slope.at[z + s], outs[1].at[z + s]))
        wait(leaving)

    return manual(
        body, name, scalars, rows.args + weights.args, [shape((NZ, count, cols), BF16)] * 2,
        [vmem((count, rows.width)), weights.scratch, vmem((NZ, BIAS_ROWS, cols)), vmem((NZ, count, cols)), vmem((NZ, count, cols))],
        rows.copies + NZ + weights.copies + 2 * NZ, after, hold,
    )


def feed_back(scalars, rows, slope, down, up, nodes, swapped, name, after=(), hold=()):
    count, cols, width = rows.count, down.cols, rows.width

    def body(sc, ins, outs, scratch, copies):
        x, wd, wu, steep, du, gb, total, parts = scratch
        row_refs, ins = take(ins, len(rows.args))
        slope_ref, ins = ins[0], ins[1:]
        down_refs, up_refs = take(ins, len(down.args))
        started = rows.load(copies, row_refs, x, sc)
        down_slots = down.load(copies, down_refs, wd, sc)
        steep_slots = [copies.start(slope_ref.at[z], steep.at[z]) for z in range(NZ)]
        up_slots = up.load(copies, up_refs, wu, sc)
        wait(started)
        leaving = []
        step = slots_at_once(cols)
        for z in range(0, NZ, step):
            for s in range(z, z + step):
                wait(down_slots[s])
                steep_slots[s].wait()
            value = nn(x[...], down.slots(wd, z, step))
            for s in range(step):
                grad = value[:, s * cols : (s + 1) * cols] * steep[z + s].astype(F32)
                gb[z + s : z + s + 1, :] = jnp.sum(grad, axis=0, keepdims=True)
                du[z + s] = grad.astype(BF16)
                leaving.append(copies.start(du.at[z + s], outs[0].at[z + s]))
        leaving.append(copies.start(gb, outs[1]))
        for z in range(NZ):
            wait(up_slots[z])
        total[...] = nt(jnp.concatenate([du[z] for z in range(NZ)], axis=1), wu[...])
        wait(leaving + store_parts(total, parts, nodes, copies, outs[2:], sc, False, swapped))

    out = manual(
        body, name, scalars, rows.args + [slope] + down.args + up.args,
        [shape((NZ, count, cols), BF16), shape((NZ, cols), F32)] + [shape((count // nodes, width), BF16)] * nodes,
        [vmem((count, width)), down.scratch, up.scratch, vmem((NZ, count, cols)), vmem((NZ, count, cols)),
         vmem((NZ, cols), F32), vmem((count, width), F32), vmem((nodes, count // nodes, width))],
        rows.copies + down.copies + up.copies + 2 * NZ + 1 + nodes, after, hold,
    )
    return out[0], out[1], list(out[2 : 2 + nodes]), out[2 + nodes :]


def feed_out(scalars, hidden, down, nodes, swapped, name, after=(), hold=()):
    _, count, cols = hidden.shape
    width = down.depth

    def body(sc, ins, outs, scratch, copies):
        y, w, total, parts = scratch
        started = [copies.start(ins[0].at[z], y.at[z]) for z in range(NZ)]
        by_slot = down.load(copies, ins[1:], w, sc)
        wait(started)
        for z in range(NZ):
            wait(by_slot[z])
        total[...] = nt(jnp.concatenate([y[z] for z in range(NZ)], axis=1), w[...])
        wait(store_parts(total, parts, nodes, copies, outs, sc, False, swapped))

    return manual(
        body, name, scalars, [hidden] + down.args, [shape((count // nodes, width), BF16)] * nodes,
        [vmem((NZ, count, cols)), down.scratch, vmem((count, width), F32), vmem((nodes, count // nodes, width))],
        NZ + down.copies + nodes, after, hold,
    )


def head_mask(cols, head):
    lane = lax.broadcasted_iota(jnp.int32, (1, cols), 1)
    return (lane >= head * HD) & (lane < (head + 1) * HD)


def attend(q, k, v):
    cols = q.shape[1]
    q = q * (1.0 / math.sqrt(HD))
    total = None
    for head in range(cols // HD):
        mask = head_mask(cols, head)
        scores = nt(jnp.where(mask, q, 0).astype(BF16), k)
        raised = jnp.exp(scores - jnp.max(scores, axis=1, keepdims=True))
        soft = raised * (1.0 / jnp.sum(raised, axis=1, keepdims=True))
        mixed = nn(soft.astype(BF16), jnp.where(mask, v, 0).astype(BF16))
        total = mixed if total is None else total + mixed
    return total.astype(BF16)


def attend_back(q, k, v, do):
    cols = q.shape[1]
    q = (q * (1.0 / math.sqrt(HD))).astype(BF16)
    dq = dk = dv = None
    for head in range(cols // HD):
        mask = head_mask(cols, head)
        qh = jnp.where(mask, q, 0).astype(BF16)
        doh = jnp.where(mask, do, 0).astype(BF16)
        kh = jnp.where(mask, k, 0).astype(BF16)
        scores = nt(k, qh)
        raised = jnp.exp(scores - jnp.max(scores, axis=0, keepdims=True))
        soft = raised * (1.0 / jnp.sum(raised, axis=0, keepdims=True))
        dsoft = nt(v, doh)
        dot = jnp.sum(dsoft * soft, axis=0, keepdims=True)
        dscores = (soft * (dsoft - dot)).astype(BF16)
        dvh = nn(soft.astype(BF16), doh)
        dkh = nn(dscores, qh)
        dqh = tn(dscores, kh)
        dq = dqh if dq is None else dq + dqh
        dk = dkh if dk is None else dk + dkh
        dv = dvh if dv is None else dv + dvh
    return (dq * (1.0 / math.sqrt(HD))).astype(BF16), dk.astype(BF16), dv.astype(BF16)


def whole_image(sc):
    return pl.ds(pl.multiple_of(sc[2] * (SEQ // 2), 32), SEQ)


def split_rows(sc):
    return pl.ds(pl.multiple_of((1 - sc[2]) * SEQ, 32), SEQ // 2)


def own_slot(dims):
    return pl.BlockSpec((1,) + dims, lambda s, *_: (2 * s, 0, 0))


def attend_whole(scalars, qkv, after=(), hold=()):
    slots, count, triple = qkv.shape
    cols = triple // 3

    def body(sc, qkv_ref, o_ref):
        rows = whole_image(sc)
        q, k, v = (qkv_ref[0, rows, j * cols : (j + 1) * cols] for j in range(3))
        o_ref[0] = attend(q, k, v)

    return call(
        body, "attend_whole", (slots,), scalars, [slot((count, triple))], slot((SEQ, cols)),
        shape((slots, SEQ, cols), BF16), [qkv],
        after=after, hold=hold, nbytes=2 * slots * count * 4 * cols,
    )


def attend_split(scalars, qkv, partner, after=(), hold=()):
    slots, half, triple = partner.shape
    count = qkv.shape[1]
    cols = triple // 3

    def body(sc, qkv_ref, partner_ref, mine_ref, theirs_ref, joined):
        joined[:half, :] = qkv_ref[0, split_rows(sc), :]
        joined[half:, :] = partner_ref[0]
        q, k, v = (joined[:, j * cols : (j + 1) * cols] for j in range(3))
        mixed = attend(q, k, v)
        mine_ref[0] = mixed[:half]
        theirs_ref[0] = mixed[half:]

    return call(
        body, "attend_split", (slots,), scalars, [own_slot((count, triple)), slot((half, triple))],
        [slot((half, cols))] * 2, [shape((slots, half, cols), BF16)] * 2, [qkv, partner],
        scratch=[pltpu.VMEM((2 * half, triple), BF16)],
        after=after, hold=hold, nbytes=2 * slots * count * 4 * cols,
    )


def attend_whole_back(scalars, qkv, do, after=(), hold=()):
    slots, count, triple = qkv.shape
    cols = triple // 3

    def body(sc, qkv_ref, do_ref, out_ref):
        rows = whole_image(sc)
        q, k, v = (qkv_ref[0, rows, j * cols : (j + 1) * cols] for j in range(3))
        grads = attend_back(q, k, v, do_ref[0, rows, :])
        for j in range(3):
            out_ref[0, :, j * cols : (j + 1) * cols] = grads[j]

    return call(
        body, "attend_whole_back", (slots,), scalars, [slot((count, triple)), slot((count, cols))],
        slot((SEQ, triple)), shape((slots, SEQ, triple), BF16), [qkv, do],
        after=after, hold=hold, nbytes=2 * slots * count * 7 * cols,
    )


def attend_split_back(scalars, qkv, partner, do, do_partner, after=(), hold=()):
    slots, half, triple = partner.shape
    count = qkv.shape[1]
    cols = triple // 3

    def body(sc, qkv_ref, partner_ref, do_ref, do_partner_ref, mine_ref, theirs_ref, joined, joined_do):
        joined[:half, :] = qkv_ref[0, split_rows(sc), :]
        joined[half:, :] = partner_ref[0]
        joined_do[:half, :] = do_ref[0, split_rows(sc), :]
        joined_do[half:, :] = do_partner_ref[0]
        q, k, v = (joined[:, j * cols : (j + 1) * cols] for j in range(3))
        grads = attend_back(q, k, v, joined_do[...])
        for j in range(3):
            mine_ref[0, :, j * cols : (j + 1) * cols] = grads[j][:half]
            theirs_ref[0, :, j * cols : (j + 1) * cols] = grads[j][half:]

    return call(
        body, "attend_split_back", (slots,), scalars,
        [own_slot((count, triple)), slot((half, triple)), own_slot((count, cols)), slot((half, cols))],
        [slot((half, triple))] * 2, [shape((slots, half, triple), BF16)] * 2, [qkv, partner, do, do_partner],
        scratch=[pltpu.VMEM((2 * half, triple), BF16), pltpu.VMEM((2 * half, cols), BF16)],
        after=after, hold=hold, nbytes=2 * slots * count * 7 * cols,
    )


def row_tile(count):
    return count // 3 if (count // 3) % 16 == 0 else count


def tiles(rows, width):
    return pl.BlockSpec((rows, width), lambda i, *_: (i, 0))


def to_relative(sc, scratch, out_ref, block):
    dps = scratch.shape[1] // block
    for k in range(dps):
        out_ref[:, k * block : (k + 1) * block] = scratch[
            :, pl.ds(pl.multiple_of((sc[0] ^ k) * block, block), block)
        ].astype(out_ref.dtype)


def from_relative(sc, refs, scratch, block):
    dps = scratch.shape[1] // block
    for k in range(dps):
        here = slice(k * block, (k + 1) * block)
        piece = refs[0][:, here].astype(F32)
        for ref in refs[1:]:
            piece += ref[:, here].astype(F32)
        scratch[:, pl.ds(pl.multiple_of((sc[0] ^ k) * block, block), block)] = piece


def normed(rows):
    centred = rows - jnp.mean(rows, axis=-1, keepdims=True)
    inverse = lax.rsqrt(jnp.mean(centred * centred, axis=-1, keepdims=True) + 1e-06)
    return centred * inverse, inverse


def norm_back(hat, inverse, grad, gain):
    scaled = grad * gain
    return inverse * (
        scaled - jnp.mean(scaled, axis=-1, keepdims=True) - hat * jnp.mean(scaled * hat, axis=-1, keepdims=True)
    )


def first_norm(scalars, tokens, cotangent, vectors, dps, after=(), hold=()):
    count, width = tokens.shape
    rows, block = row_tile(count), width // dps

    def body(sc, x_ref, cot_ref, vec_ref, a_ref, g_ref, scratch):
        hat, _ = normed(x_ref[...])
        scratch[...] = hat * vec_ref[0:1] + vec_ref[1:2]
        to_relative(sc, scratch, a_ref, block)
        to_relative(sc, cot_ref, g_ref, block)

    return call(
        body, "first_norm", (count // rows,), scalars,
        [tiles(rows, width)] * 2 + [whole(vectors.shape)], [tiles(rows, width)] * 2,
        [shape((count, width), BF16)] * 2, [tokens, cotangent, vectors],
        scratch=[pltpu.VMEM((rows, width), F32)], after=after, hold=hold, nbytes=12 * count * width,
    )


def second_norm(scalars, tokens, parts, vectors, dps, after=(), hold=()):
    count, width = tokens.shape
    rows, block = row_tile(count), width // dps

    def body(sc, x_ref, vec_ref, *refs):
        h_ref, c_ref, scratch = refs[-3:]
        from_relative(sc, refs[:-3], scratch, block)
        h = x_ref[...] + scratch[...] + vec_ref[4:5]
        h_ref[...] = h
        hat, _ = normed(h)
        scratch[...] = hat * vec_ref[2:3] + vec_ref[3:4]
        to_relative(sc, scratch, c_ref, block)

    return call(
        body, "second_norm", (count // rows,), scalars,
        [tiles(rows, width), whole(vectors.shape)] + [tiles(rows, width)] * len(parts), [tiles(rows, width)] * 2,
        [shape((count, width), F32), shape((count, width), BF16)], [tokens, vectors] + list(parts),
        scratch=[pltpu.VMEM((rows, width), F32)], after=after, hold=hold, nbytes=14 * count * width,
    )


def layer_output(scalars, middle, parts, vectors, dps, after=(), hold=()):
    count, width = middle.shape
    rows, block = row_tile(count), width // dps

    def body(sc, h_ref, vec_ref, *refs):
        out_ref, scratch = refs[-2:]
        from_relative(sc, refs[:-2], scratch, block)
        out_ref[...] = h_ref[...] + scratch[...] + vec_ref[5:6]

    return call(
        body, "layer_output", (count // rows,), scalars,
        [tiles(rows, width), whole(vectors.shape)] + [tiles(rows, width)] * len(parts), tiles(rows, width),
        shape((count, width), F32), [middle, vectors] + list(parts),
        scratch=[pltpu.VMEM((rows, width), F32)], after=after, hold=hold, nbytes=12 * count * width,
    )


def add_rows(ref, values):
    step = pl.program_id(0)

    @pl.when(step == 0)
    def _():
        ref[...] = values

    @pl.when(step > 0)
    def _():
        ref[...] += values


def second_norm_back(scalars, middle, cotangent, parts, vectors, dps, after=(), hold=()):
    count, width = middle.shape
    rows, block = row_tile(count), width // dps

    def body(sc, h_ref, cot_ref, vec_ref, *refs):
        dh_ref, e_ref, sums_ref, scratch = refs[-4:]
        from_relative(sc, refs[:-4], scratch, block)
        dc = scratch[...]
        hat, inverse = normed(h_ref[...])
        cot = cot_ref[...]
        dh = cot + norm_back(hat, inverse, dc, vec_ref[2:3])
        dh_ref[...] = dh
        scratch[...] = dh
        to_relative(sc, scratch, e_ref, block)
        column = lambda values: jnp.sum(values, axis=0, keepdims=True)
        add_rows(sums_ref, jnp.concatenate([column(dc * hat), column(dc), column(dh), column(cot)], axis=0))

    return call(
        body, "second_norm_back", (count // rows,), scalars,
        [tiles(rows, width)] * 2 + [whole(vectors.shape)] + [tiles(rows, width)] * len(parts),
        [tiles(rows, width)] * 2 + [whole((4, width))],
        [shape((count, width), F32), shape((count, width), BF16), shape((4, width), F32)],
        [middle, cotangent, vectors] + list(parts),
        scratch=[pltpu.VMEM((rows, width), F32)], after=after, hold=hold, nbytes=18 * count * width,
    )


def first_norm_back(scalars, tokens, middle_grad, parts, vectors, dps, after=(), hold=()):
    count, width = tokens.shape
    rows, block = row_tile(count), width // dps

    def body(sc, x_ref, dh_ref, vec_ref, *refs):
        dx_ref, sums_ref, scratch = refs[-3:]
        from_relative(sc, refs[:-3], scratch, block)
        da = scratch[...]
        hat, inverse = normed(x_ref[...])
        dx_ref[...] = dh_ref[...] + norm_back(hat, inverse, da, vec_ref[0:1])
        column = lambda values: jnp.sum(values, axis=0, keepdims=True)
        add_rows(sums_ref, jnp.concatenate([column(da * hat), column(da)], axis=0))

    return call(
        body, "first_norm_back", (count // rows,), scalars,
        [tiles(rows, width)] * 2 + [whole(vectors.shape)] + [tiles(rows, width)] * len(parts),
        [tiles(rows, width), whole((2, width))],
        [shape((count, width), F32), shape((2, width), F32)], [tokens, middle_grad, vectors] + list(parts),
        scratch=[pltpu.VMEM((rows, width), F32)], after=after, hold=hold, nbytes=16 * count * width,
    )


def adam_step(weight, gradient, first, second, rate, decay):
    first = 0.9 * first + 0.1 * gradient
    second = 0.999 * second + 0.001 * gradient * gradient
    first_fix = 1.0 - 0.9**STEP
    second_fix = 1.0 - 0.999**STEP
    update = first / first_fix / (jnp.sqrt(second / second_fix) + 1e-08) + decay * weight
    return (gradient, first, second, weight - rate * update)


def by_part(columns, heads):
    return jnp.concatenate([columns[:, (h * 3 + c) * HD : (h * 3 + c + 1) * HD] for c in range(3) for h in range(heads)], axis=1)


def by_head(columns, heads):
    return jnp.concatenate([columns[:, (c * heads + h) * HD : (c * heads + h + 1) * HD] for h in range(heads) for c in range(3)], axis=1)


def plain(body, name, args, out_shape, after=(), hold=()):
    given, extra = len(args), len(after) + len(hold)
    made = len(out_shape)
    nbytes = sum(math.prod(a.shape) * a.dtype.itemsize for a in list(args) + list(out_shape))

    def run(*refs):
        body(*refs[:given], *refs[given + extra : given + extra + made])

    anywhere = pl.BlockSpec(memory_space=pltpu.HBM)
    here = pl.BlockSpec(memory_space=pltpu.VMEM)
    first = given + len(after)
    return pl.pallas_call(
        run, name=name,
        out_shape=list(out_shape) + [shape(h.shape, h.dtype) for h in hold],
        in_specs=[pl.BlockSpec(memory_space=pltpu.SMEM)] + [here] * (given - 1) + [anywhere] * extra,
        out_specs=[here] * made + [anywhere] * len(hold),
        input_output_aliases={first + i: made + i for i in range(len(hold))},
        compiler_params=pltpu.CompilerParams(vmem_limit_bytes=VMEM_LIMIT), cost_estimate=cost(name, nbytes),
    )(*args, *after, *hold)


def attn_piece(scalars, w_qkv, w_out):
    heads = w_qkv.shape[1] // (3 * HD)
    triple = w_qkv.shape[1]

    def body(sc, qkv_ref, out_ref, piece_ref):
        piece_ref[:, :triple] = by_part(qkv_ref[...], heads).astype(BF16)
        piece_ref[:, triple:] = out_ref[...].T.astype(BF16)

    return plain(body, "attn_piece", [scalars, w_qkv, w_out], [shape((w_qkv.shape[0], triple + w_out.shape[0]), BF16)])[0]


def hidden_pieces(scalars, w_up, hidden_bias, w_down, after=()):
    block, cols = w_up.shape[0], w_up.shape[1] // 2

    def body(sc, up_ref, bias_ref, down_ref, my_up_ref, my_down_ref, theirs_ref):
        mine, other = (pl.ds(pl.multiple_of(h * cols, cols), cols) for h in (sc[4], 1 - sc[4]))
        my_up_ref[:block, :] = up_ref[:, mine].astype(BF16)
        my_down_ref[...] = down_ref[mine, :].T.astype(BF16)
        theirs_ref[:block, :] = up_ref[:, other].astype(BF16)
        theirs_ref[block:, :] = down_ref[other, :].T.astype(BF16)
        rest = bias_ref[:, mine]
        row = lax.broadcasted_iota(jnp.int32, (BIAS_ROWS, cols), 0)
        terms = jnp.zeros((BIAS_ROWS, cols), F32)
        for i in range(3):
            term = rest.astype(BF16).astype(F32)
            terms = jnp.where(row == i, term, terms)
            rest = rest - term
        my_up_ref[block:, :] = terms.astype(BF16)

    return plain(
        body, "hidden_pieces", [scalars, w_up, hidden_bias[None, :], w_down],
        [shape((block + BIAS_ROWS, cols), BF16), shape((block, cols), BF16), shape((2 * block, cols), BF16)], after,
    )


def attn_adam(scalars, sums, w_qkv, qkv_m, qkv_v, w_out, out_m, out_v, after=()):
    heads, triple = w_qkv.shape[1] // (3 * HD), w_qkv.shape[1]
    count = len(sums)

    def body(sc, *refs):
        total = None
        for ref in refs[:count]:
            piece = (ref[0] if len(ref.shape) == 3 else ref[...]).astype(F32)
            total = piece if total is None else total + piece
        qw, qm, qv, ow, om, ov = (r[...] for r in refs[count : count + 6])
        outs = refs[count + 6 :]
        new = adam_step(qw, by_head(total[:, :triple], heads), qm, qv, 0.1, 0.05)
        new += adam_step(ow, total[:, triple:].T, om, ov, 0.2, 0.05)
        for ref, value in zip(outs, new):
            ref[...] = value

    out = plain(
        body, "attn_adam", [scalars] + list(sums) + [w_qkv, qkv_m, qkv_v, w_out, out_m, out_v],
        [shape(w_qkv.shape, F32)] * 4 + [shape(w_out.shape, F32)] * 4, after,
    )
    return tuple(out[:4]), tuple(out[4:])


def hidden_adam(scalars, up_total, down_total, far, up, down, after=(), hold=()):
    block, cols = far.shape[0] // 2, far.shape[1]

    def body(sc, up_total_ref, down_total_ref, far_ref, *refs):
        ins, outs = take(refs, 6)
        up_grad, down_grad = outs[0], outs[4]
        mine, other = (pl.ds(pl.multiple_of(h * cols, cols), cols) for h in (sc[4], 1 - sc[4]))
        up_grad[:, mine] = up_total_ref[:block, :].astype(F32)
        up_grad[:, other] = far_ref[:block, :].astype(F32)
        down_grad[mine, :] = down_total_ref[:block, :].astype(F32).T
        down_grad[other, :] = far_ref[block:, :].astype(F32).T
        for (w, m, v), made, rate in ((ins[:3], outs[:4], 0.1), (ins[3:], outs[4:], 0.05)):
            new = adam_step(w[...], made[0][...], m[...], v[...], rate, 0.05)
            for ref, value in zip(made[1:], new[1:]):
                ref[...] = value

    out = plain(
        body, "hidden_adam", [scalars, up_total, down_total, far] + list(up) + list(down),
        [shape(up[0].shape, F32)] * 4 + [shape(down[0].shape, F32)] * 4, after, hold,
    )
    return tuple(out[:4]), tuple(out[4:8]), out[8:]


def solution(mesh):
    dps, tensor = mesh.shape["dp"], mesh.shape["tensor"]
    nodes = tensor // NZ
    devices = dps * tensor
    z_groups = [
        [d * tensor + z * nodes + c for z in range(NZ)] for d in range(dps) for c in range(nodes)
    ]

    def swap(value, flip):
        return lax.ppermute(value, AXES, [(i, i ^ flip) for i in range(devices)])

    def gather_z(piece):
        return lax.all_gather(piece, AXES, axis=0, axis_index_groups=z_groups)

    def scatter_z(total):
        return lax.psum_scatter(total, AXES, scatter_dimension=0, axis_index_groups=z_groups, tiled=True)[0]

    def by_weight(k):
        return (bin(k).count("1"), k)

    def gather(own, count, unit, low_first):
        bufs = [own] + [None] * (count - 1)
        for k in sorted(range(1, count), key=by_weight):
            last = k & -k if low_first else 1 << (k.bit_length() - 1)
            bufs[k] = swap(bufs[k ^ last], last * unit)
        return bufs

    def plus(left, right):
        return (left.astype(F32) + right.astype(F32)).astype(BF16)

    def scatter(bufs, unit, low_first):
        bufs, sums = list(bufs), [bufs[0]]
        for k in sorted(range(1, len(bufs)), key=by_weight, reverse=True):
            last = k & -k if low_first else 1 << (k.bit_length() - 1)
            arrived = swap(bufs[k], last * unit)
            if k == last:
                sums.append(arrived)
            else:
                bufs[k ^ last] = plus(bufs[k ^ last], arrived)
        return sums

    def add_up(sums):
        total = sums[0].astype(F32)
        for piece in sums[1:]:
            total = total + piece.astype(F32)
        return total.astype(BF16)

    def along_z(piece):
        return [piece] + [swap(piece, j * nodes) for j in range(1, NZ)]

    def relative(own):
        return [own] + [swap(own, j) for j in range(1, nodes)]

    def ordered_rows(parts, member):
        if parts[0].shape[0] % 16 == 0:
            return Rows(parts, True)
        flip = 1
        while len(parts) > 1:
            odd = (member // flip) % 2 == 1
            parts = [
                jnp.where(odd, jnp.concatenate([b, a], axis=0), jnp.concatenate([a, b], axis=0))
                for a, b in zip(parts[0::2], parts[1::2])
            ]
            flip *= 2
        return Rows(parts, True)

    def relative_rows(parts, swapped=0):
        if parts[0].shape[0] % 16:
            parts = [jnp.concatenate(parts, axis=0)]
        return Rows(parts, False, swapped)

    def send_parts(parts):
        return [parts[0]] + [swap(parts[j], j) for j in range(1, nodes)]

    def per_device(
        tokens, cotangent, vectors, vectors_m, vectors_v,
        w_qkv, qkv_m, qkv_v, w_out, out_m, out_v, w_up, up_m, up_v,
        hidden_bias, bias_m, bias_v, w_down, down_m, down_v,
    ):
        dp_index = lax.axis_index("dp")
        tensor_index = lax.axis_index("tensor")
        z_index, member = tensor_index // nodes, tensor_index % nodes
        odd_x = dp_index % 2
        scalars = jnp.stack([dp_index, member, z_index % 2, z_index, odd_x]).astype(jnp.int32)
        block = w_qkv.shape[0]
        triple, width = w_qkv.shape[1], w_out.shape[0]
        hidden_here = w_up.shape[1] // 2

        attn_z = along_z(attn_piece(scalars, w_qkv, w_out))
        my_up, my_down, theirs = hidden_pieces(scalars, w_up, hidden_bias, w_down, after=[attn_z[0]])
        arrived = swap(theirs, tensor)
        (lower,) = pack(scalars, attn_z[:2], after=[my_up])
        lowers = gather(lower, dps, tensor, False)
        up_piece = jnp.concatenate([my_up, arrived[:block]], axis=0)
        down_piece = jnp.concatenate([my_down, arrived[block:]], axis=0)
        down_piece = jnp.concatenate(gather(down_piece, dps // 2, 2 * tensor, False), axis=0)
        upper, up_piece, down_piece = pack(scalars, attn_z[2:], after=[lower], hold=[up_piece, down_piece])
        uppers = gather(upper, dps, tensor, True)
        a_own, g_own = first_norm(scalars, tokens, cotangent, vectors, dps, after=[upper] + lowers[1:3])
        a_parts = relative(a_own)
        up_z = gather_z(up_piece)
        halves = [(0, [(2 * k + z // 2, z % 2) for z in range(NZ)]) for k in range(dps)]
        attn_w = [half for pair in zip(lowers, uppers) for half in pair]
        qkv_w = Weights(attn_w, halves, block, 0, triple)
        out_w = Weights(attn_w, halves, block, triple, width)

        a_rows = ordered_rows(a_parts, member)
        qkv, qkv_theirs, g_own, up_z = project(scalars, a_rows, qkv_w, "qkv", hold=[g_own, up_z])
        qkv_partner = swap(qkv_theirs, nodes)
        g_far = swap(g_own, tensor)
        mixed = attend_whole(scalars, qkv)

        up_rows = [(0, block + BIAS_ROWS)[k % 2] for k in range(dps)]
        up_w = Weights(
            gather(up_z, dps // 2, 2 * tensor, False), [(row, [(k // 2, None)] * NZ) for k, row in enumerate(up_rows)],
            block, 0, hidden_here,
        )
        mixed_mine, mixed_theirs, down_piece = attend_split(scalars, qkv, qkv_partner, after=[mixed], hold=[down_piece])
        mixed = SplitSlots(mixed, mixed_mine, swap(mixed_theirs, nodes))
        *attn_parts, g_far = project_back(
            scalars, mixed, out_w, nodes, "attn_out", after=up_w.args[1:], hold=[g_far]
        )
        middle, c_own = second_norm(scalars, tokens, send_parts(attn_parts), vectors, dps)
        down_w = Weights(
            [gather_z(down_piece)], [(k * block, [(0, None)] * NZ) for k in range(dps)], block, 0, hidden_here
        )

        c_far = swap(c_own, tensor)
        g_rows, g_far = relative_rows(relative(g_own)), relative_rows(relative(g_far), dps)
        c_rows = relative_rows(relative(c_own))
        hidden, slope = feed_forward(scalars, c_rows, up_w, block, "feed_forward")
        (c_far,) = gate(scalars, [hidden], [c_far])
        c_far = relative_rows(relative(c_far), dps)
        hidden_far, slope_far = feed_forward(scalars, c_far, up_w, block, "feed_forward_far", after=[hidden])
        du, bias_near, dc_near, _ = feed_back(
            scalars, g_rows, slope, down_w, up_w, nodes, 0, "feed_back", after=[hidden_far]
        )
        dc_near = send_parts(dc_near)
        du_far, bias_far, dc_far, _ = feed_back(
            scalars, g_far, slope_far, down_w, up_w, nodes, dps, "feed_back_far", after=[du]
        )
        (dc_sum,) = add(scalars, send_parts(dc_far), after=[du_far])
        dc_arrived = swap(dc_sum, tensor)

        def hidden_goal(sc, outs, part, k, z):
            if part == 0:
                return outs[0].at[sc[3] ^ z, pl.ds(k * block, block), :]
            return outs[1 + k // 2].at[sc[3] ^ z, pl.ds((k % 2) * block, block), :]

        down_part, *up_part = weight_grads(
            scalars,
            [([g_rows, g_far], [Slots(hidden), Slots(hidden_far)]), ([c_rows, c_far], [Slots(du), Slots(du_far)])],
            dps, [shape((NZ, rows * block, hidden_here), BF16) for rows in [dps] + [2] * (dps // 2)],
            hidden_goal, False, "hidden_grad", after=[dc_sum] + dc_near[1:],
        )
        down_part = scatter_z(down_part)
        out_far = feed_out(scalars, hidden_far, down_w, nodes, dps, "feed_out_far", after=[up_part[0]])
        middle_grad, e_own, sums_two = second_norm_back(
            scalars, middle, cotangent, dc_near + [dc_arrived], vectors, dps, after=[out_far[0]]
        )
        out_far = send_parts(out_far)

        e_rows = ordered_rows(relative(e_own), member)
        dmixed, dmixed_theirs, out_far[0] = project(
            scalars, e_rows, out_w, "mixed_grad", after=out_far[1:], hold=[out_far[0]]
        )
        dmixed_partner = swap(dmixed_theirs, nodes)
        out_arrived = swap(add_up(out_far), tensor)
        out_near = feed_out(scalars, hidden, down_w, nodes, 0, "feed_out", after=[dmixed])
        dqkv_mine, dqkv_theirs = attend_split_back(
            scalars, qkv, qkv_partner, dmixed, dmixed_partner, after=[out_near[0]]
        )
        dqkv, down_part = attend_whole_back(scalars, qkv, dmixed, after=[dqkv_mine], hold=[down_part])
        down_part = scatter([down_part[2 * j * block : 2 * (j + 1) * block] for j in range(dps // 2)], 2 * tensor, False)
        dqkv = SplitSlots(dqkv, dqkv_mine, swap(dqkv_theirs, nodes))

        def attn_goal(sc, outs, part, k, z):
            return outs[2 * k + z // 2].at[z % 2]

        da_parts = send_parts(project_back(scalars, dqkv, qkv_w, nodes, "first_back", after=[out_arrived]))
        *attn_part, up_part[0], down_part[0] = weight_grads(
            scalars, [([a_rows], [dqkv]), ([e_rows], [mixed])],
            dps, [shape((NZ // 2, block, triple + width), BF16)] * (2 * dps), attn_goal, True, "attn_grad",
            after=[da_parts[0]] + down_part[1:], hold=[up_part[0], down_part[0]],
        )
        down_part = add_up(down_part)
        lowers, uppers = attn_part[0::2], attn_part[1::2]
        up_part = scatter_z(add_up(scatter(up_part, 2 * tensor, False)))
        input_grad, sums_one = first_norm_back(
            scalars, tokens, middle_grad, da_parts, vectors, dps, after=[attn_part[0]]
        )

        here = (jnp.arange(nodes)[:, None] == member) & (jnp.arange(2)[None, :] == odd_x)
        own_slot_of = (jnp.arange(NZ)[:, None] ^ z_index) == jnp.arange(NZ)[None, :]
        bias_here = jnp.sum(jnp.where(own_slot_of[:, :, None], (bias_near + bias_far)[None], 0.0), axis=1)
        bias_part = jnp.where(here[None, :, :, None], bias_here[:, None, None, :], 0.0)
        rows_two = sums_one.shape[0] + sums_two.shape[0]
        value = jnp.concatenate([sums_one, sums_two, bias_part.reshape(-1, sums_two.shape[1])], axis=0)
        bits = [1 << i for i in range(devices.bit_length() - 1)]
        stages = [bits[:1]] + [bits[i : i + 2] for i in range(1, len(bits), 2)] if len(bits) % 2 else [
            bits[i : i + 2] for i in range(0, len(bits), 2)
        ]

        def exchange(value, stage):
            flips = stage + [sum(stage)] if len(stage) > 1 else stage
            return [swap(value, flip) for flip in flips]

        def combine(value, arrived):
            near = value + arrived[0]
            return near + (arrived[1] + arrived[2]) if len(arrived) > 1 else near

        arrived = exchange(value, stages[0])

        if dps == 4:
            far_upper, far_lower = swap(uppers[3], tensor), swap(lowers[3], 2 * tensor)
            upper_x, lower_y = swap(uppers[1], tensor), swap(lowers[2], 2 * tensor)
            upper, lower, value = add_groups(
                scalars, [[uppers[2], far_upper], [lowers[1], far_lower]], False, after=[input_grad], hold=[value]
            )
            uppers = [uppers[0], upper_x, swap(upper, 2 * tensor)]
            lowers = [lowers[0], swap(lower, tensor), lower_y]
        else:
            uppers, lowers = scatter(uppers, tensor, True), scatter(lowers, tensor, False)
        value = combine(value, arrived)
        arrived = exchange(value, stages[1])
        output = layer_output(
            scalars, middle, send_parts(out_near) + [out_arrived], vectors, dps, after=[input_grad, uppers[0], value]
        )
        value = combine(value, arrived)
        own, *pieces, value = add_groups(scalars, [lowers, uppers], True, after=[output], hold=[value])
        sums = [own] + [swap(piece, (j + 1) * nodes) for j, piece in enumerate(pieces)]
        for stage in stages[2:]:
            value = combine(value, exchange(value, stage))
        all_sums = value
        far = swap(jnp.concatenate([up_part[block:], down_part[block:]], axis=0), tensor)
        up_res, down_res, _ = hidden_adam(
            scalars, up_part, down_part, far, (w_up, up_m, up_v), (w_down, down_m, down_v), after=[own]
        )
        qkv_res, out_res = attn_adam(scalars, sums, w_qkv, qkv_m, qkv_v, w_out, out_m, out_v, after=[up_res[0]])
        vector_total = all_sums[:rows_two]
        bias_total = lax.dynamic_slice_in_dim(
            all_sums[rows_two:].reshape(-1), tensor_index * 2 * hidden_here, 2 * hidden_here, 0
        )

        vec_res = adam_step(vectors, vector_total, vectors_m, vectors_v, 0.3, 0.0)
        bias_res = adam_step(hidden_bias, bias_total, bias_m, bias_v, 0.3, 0.0)
        return (output, input_grad) + vec_res + qkv_res + out_res + up_res + bias_res + down_res

    rows, both = P(AXES, None), P("dp", "tensor")
    turned = P("tensor", "dp")
    in_specs = (
        (rows,) * 2 + (P(),) * 3 + (both,) * 3 + (turned,) * 3 + (both,) * 3 + (P("tensor"),) * 3 + (turned,) * 3
    )
    out_specs = (
        (rows,) * 2 + (P(),) * 4 + (both,) * 4 + (turned,) * 4 + (both,) * 4 + (P("tensor"),) * 4 + (turned,) * 4
    )
    return jax.shard_map(per_device, mesh=mesh, in_specs=in_specs, out_specs=out_specs, check_vma=False)
```

time: 944 us -> 396 us (0.42)
  waiting for transfers between devices: 595 us -> 109 us
  Pallas kernels: 0 us -> 189 us
  matrix products: 131 us -> 0 us
  blocking collectives: 65.3 us -> 0 us
  local copies, waits for them, and re-layouts: 65.9 us -> 14.7 us
  other arithmetic: 55.3 us -> 16 us
  starting transfers between devices: 7.96 us -> 45 us
    reduce_scatter x7 -> x2, waiting for transfers between devices: 313 us -> 0.02 us  [scatter_z(): lax.psum_scatter(total, AXES, scatter_dimension=0, axis_index_groups=z_gr...]
    all_gather x7 -> x2, waiting for transfers between devices: 262 us -> 0.02 us  [gather_z(): return lax.all_gather(piece, AXES, axis=0, axis_index_groups=z_groups)]
    pallas_call x0 -> x31, Pallas kernels: none -> 189 us  [the longest x18 110 us: manual(): pl.pallas_call(run, name=name, in_specs=[pl.BlockSpec(memory_space=pltpu....]
    dot_general x54 -> x0, matrix products: 131 us -> none  [the longest x4 44.9 us: outer_cols(): lax.dot_general(left, right, (((1,), (1,)), ((), ())), preferred_element_...]
    ppermute x0 -> x51, waiting for transfers between devices: none -> 108 us  [swap(): return lax.ppermute(value, AXES, [(i, i ^ flip) for i in range(devices)])]
    ppermute x0 -> x51, starting transfers between devices: none -> 44.9 us  [swap(): return lax.ppermute(value, AXES, [(i, i ^ flip) for i in range(devices)])]
    psum x1 -> x0, blocking collectives: 43.6 us -> none  [per_device(): lax.psum((vector_part, bias_padded), ('dp', 'tensor'))]
    all_gather x2 -> x0, blocking collectives: 21.6 us -> none  [the longest x1 10.9 us: per_device(): lax.all_gather(w_qkv.astype(jnp.bfloat16), 'dp', axis=0, tiled=True)]
  transfers between devices with their start and end apart: 15 -> 55, of which waited for: 12 -> 25; matrix products, arithmetic and copies ran while one was open for 21% -> 5% of each run, Pallas kernels for 0% -> 39%
where the time goes in v1:
time: 396 us; the launch traced here: 388 us
  Pallas kernels  189 us (48%)
  waiting for transfers between devices  109 us (28%)
  starting transfers between devices  45 us (11%)
  other arithmetic  16 us (4%)
  between operations  15 us (4%)
  local copies, waits for them, and re-layouts  14.7 us (4%)
    pallas_call x18, Pallas kernels, manual(): pl.pallas_call(run, name=name, in_specs=[pl.BlockSpec(memory_space=pltpu....  110 us
    ppermute x51, waiting for transfers between devices, swap(): return lax.ppermute(value, AXES, [(i, i ^ flip) for i in range(devices)])  108 us
    pallas_call x9, Pallas kernels, call(): pl.pallas_call(run, name=name, grid_spec=pltpu.PrefetchScalarGridSpec(num...  66.3 us
    ppermute x51, starting transfers between devices, swap(): return lax.ppermute(value, AXES, [(i, i ^ flip) for i in range(devices)])  44.9 us
    pallas_call x4, Pallas kernels, plain(): pl.pallas_call(run, name=name, out_shape=list(out_shape) + [shape(h.shape...  12.1 us
    unnamed x70, local copies, waits for them, and re-layouts  10.5 us
  transfers between devices with their start and end apart: 55, of which 25 were waited for; matrix products, arithmetic and copies ran while one was open for 5% of the time, Pallas kernels for 39%

profile of v1, /device:TPU:10, one launch (start us, length us, event | category | flops | bytes accessed | tf_op | source)
XLA Modules:
  0.0 387.9 jit_solution(7565073308199260677)
XLA Ops:
  8.0 1.9 attn_piece.1.refs_4_.refs_0_
  9.9 2.1 hidden_pieces.1
  12.5 7.7 %collective-permute-done.3 = bf16[512,256]{1,0:T(8,128)(2,1)S(1)} collective-permute-done((bf16[512,256]{1,0:T(8,128)(2,1)}, bf16[512,256]{1,0:T(8,128)(2,1)S(1)}, u32[]{:S(2)}, u32[]{:S(2)}) %collective-permute-start.3) | collective-permute-done | bytes 262176 | tf_op jit(solution)/shard_map/ppermute | solution.py:941
  20.9 1.6 pad_maximum_fusion.2
  27.6 2.4 pack.2.refs_2_.refs_3_
  30.9 1.7 pad_maximum_fusion.1.refs_3_
  32.6 1.8 pad_maximum_fusion.refs_4_
  34.4 8.9 %collective-permute-done.1.refs_1_ = bf16[256,512]{1,0:T(8,128)(2,1)} collective-permute-done((bf16[256,512]{1,0:T(8,128)(2,1)S(1)}, bf16[256,512]{1,0:T(8,128)(2,1)}, u32[]{:S(2)}, u32[]{:S(2)}) %collective-permute-start.1) | collective-permute-done | bytes 262176 | tf_op jit(solution)/shard_map/ppermute | solution.py:941
  43.4 3.5 collective-permute-done.refs_0_
  46.9 2.4 pack.3
  50.8 5.0 %first_norm.1 = (bf16[432,1024]{1,0:T(8,128)(2,1)}, bf16[432,1024]{1,0:T(8,128)(2,1)}) custom-call(s32[5]{0:T(128)} %stack.23.refs_0_.sc, f32[432,1024]{1,0:T(8,128)} %refs_0_.5, f32[432,1024]{1,0:T(8,128)} %refs_1_.10, f32[6,1024]{1,0:T(8,128)} %refs_1_.11, bf16[2,256,512]{2,1,0:T(8,128)(2,1)} %get-tuple-element.116.refs_3_.refs_4_, ...), custom_call_target="tpu_custom_call" | custom-call | flops 2500000000 | bytes 5308416 | tf_op jit(solution)/shard_map/first_norm/pallas_call | solution.py:50
  58.0 5.8 %collective-permute-done.9.refs_7_.refs_8_ = bf16[2,256,512]{2,1,0:T(8,128)(2,1)} collective-permute-done((bf16[2,256,512]{2,1,0:T(8,128)(2,1)}, bf16[2,256,512]{2,1,0:T(8,128)(2,1)}, u32[]{:S(2)}, u32[]{:S(2)}) %collective-permute-start.9) | collective-permute-done | bytes 524320 | tf_op jit(solution)/shard_map/ppermute | solution.py:941
  63.8 7.1 %collective-permute-done.8.refs_5_.refs_6_ = bf16[2,256,512]{2,1,0:T(8,128)(2,1)S(1)} collective-permute-done((bf16[2,256,512]{2,1,0:T(8,128)(2,1)}, bf16[2,256,512]{2,1,0:T(8,128)(2,1)S(1)}, u32[]{:S(2)}, u32[]{:S(2)}) %collective-permute-start.8) | collective-permute-done | bytes 524320 | tf_op jit(solution)/shard_map/ppermute | solution.py:941
  70.9 2.1 collective-permute-done.10.refs_8_.refs_9_
  72.9 8.8 %collective-permute-done.11.refs_9_.refs_10_ = bf16[2,256,512]{2,1,0:T(8,128)(2,1)} collective-permute-done((bf16[2,256,512]{2,1,0:T(8,128)(2,1)}, bf16[2,256,512]{2,1,0:T(8,128)(2,1)}, u32[]{:S(2)}, u32[]{:S(2)}) %collective-permute-start.11) | collective-permute-done | bytes 524320 | tf_op jit(solution)/shard_map/ppermute | solution.py:941
  81.7 7.4 %qkv.1 = (bf16[4,864,384]{2,1,0:T(8,128)(2,1)}, bf16[2,288,384]{2,1,0:T(8,128)(2,1)}, bf16[432,1024]{1,0:T(8,128)(2,1)}, bf16[4,528,256]{2,1,0:T(8,128)(2,1)}) custom-call(s32[5]{0:T(128)} %stack.23.refs_0_.sc, bf16[432,1024]{1,0:T(8,128)(2,1)} %get-tuple-element.117.refs_0_, ...), custom_call_target="tpu_custom_call", output_to_operand_aliasing={{2}: (11, {}), {3}: (12, {})} | custom-call | bytes 9060352 | tf_op jit(solution)/shard_map/qkv/pallas_call | solution.py:114
  90.7 2.5 collective-permute-start.12
  93.7 8.3 %attend_whole.1.refs_2_.refs_0_.refs_7_ = bf16[4,576,128]{2,1,0:T(8,128)(2,1)} custom-call(s32[5]{0:T(128)} %stack.23.refs_0_.sc, bf16[4,864,384]{2,1,0:T(8,128)(2,1)} %get-tuple-element.120.refs_0_), custom_call_target="tpu_custom_call" | custom-call | bytes 3538944 | tf_op jit(solution)/shard_map/attend_whole/pallas_call | solution.py:50
  103.2 5.4 %attend_split.1 = (bf16[2,288,128]{2,1,0:T(8,128)(2,1)}, bf16[2,288,128]{2,1,0:T(8,128)(2,1)}, bf16[1024,256]{1,0:T(8,128)(2,1)}) custom-call(s32[5]{0:T(128)} %stack.23.refs_0_.sc, bf16[4,864,384]{2,1,0:T(8,128)(2,1)} %get-tuple-element.120.refs_0_, bf16[2,288,384]{2,1,0:T(8,128)(2,1)} %collective-permute-done.12.refs_1_, ...), custom_call_target="tpu_custom_call", output_to_operand_aliasing={{2}: (4, {})} | custom-call | bytes 1769472 | tf_op jit(solution)/shard_map/attend_split/pallas_call | solution.py:50
  108.7 1.8 collective-permute-start.13
  110.6 3.6 collective-permute-done.13.refs_2_.refs_9_
  115.8 5.0 %attn_out.1 = (bf16[432,1024]{1,0:T(8,128)(2,1)}, bf16[432,1024]{1,0:T(8,128)(2,1)}, bf16[432,1024]{1,0:T(8,128)(2,1)}) custom-call(s32[5]{0:T(128)} %stack.23.refs_0_.sc, bf16[4,576,128]{2,1,0:T(8,128)(2,1)} %attend_whole.1.refs_2_.refs_0_.refs_7_, bf16[2,288,128]{2,1,0:T(8,128)(2,1)} %get-tuple-element.123.refs_1_.refs_8_, ...), custom_call_target="tpu_custom_call", output_to_operand_aliasing={{2}: (13, {})} | custom-call | bytes 6848512 | tf_op jit(solution)/shard_map/attn_out/pallas_call | solution.py:114
  120.8 2.6 collective-permute-done.16.refs_3_
  124.3 5.6 %second_norm.1 = (f32[432,1024]{1,0:T(8,128)}, bf16[432,1024]{1,0:T(8,128)(2,1)}) custom-call(s32[5]{0:T(128)} %stack.23.refs_0_.sc, f32[432,1024]{1,0:T(8,128)} %refs_0_.5, f32[6,1024]{1,0:T(8,128)} %refs_1_.11, bf16[432,1024]{1,0:T(8,128)(2,1)} %get-tuple-element.127.refs_2_, bf16[432,1024]{1,0:T(8,128)(2,1)} %copy-done.15), custom_call_target="tpu_custom_call" | custom-call | bytes 6193152 | tf_op jit(solution)/shard_map/second_norm/pallas_call | solution.py:50
  130.7 2.1 collective-permute-done.17.refs_1_.refs_7_
  132.8 7.3 %feed_forward.1 = (bf16[4,864,256]{2,1,0:T(8,128)(2,1)}, bf16[4,864,256]{2,1,0:T(8,128)(2,1)}) custom-call(s32[5]{0:T(128)} %stack.23.refs_0_.sc, bf16[432,1024]{1,0:T(8,128)(2,1)} %get-tuple-element.130.refs_0_.refs_6_, bf16[432,1024]{1,0:T(8,128)(2,1)} %collective-permute-done.17.refs_1_.refs_7_, bf16[4,528,256]{2,1,0:T(8,128)(2,1)} %get-tuple-element.125.refs_2_.refs_4_, ...), custom_call_target="tpu_custom_call" | custom-call | bytes 7471104 | tf_op jit(solution)/shard_map/feed_forward/pallas_call | solution.py:114
  140.1 12.2 %collective-permute-done.19.refs_1_ = bf16[432,1024]{1,0:T(8,128)(2,1)S(1)} collective-permute-done((bf16[432,1024]{1,0:T(8,128)(2,1)}, bf16[432,1024]{1,0:T(8,128)(2,1)S(1)}, u32[]{:S(2)}, u32[]{:S(2)}) %collective-permute-start.19) | collective-permute-done | bytes 884768 | tf_op jit(solution)/shard_map/ppermute | solution.py:941
  154.7 2.2 collective-permute-done.20.refs_1_.refs_9_
  156.9 7.5 %feed_forward_far.1 = (bf16[4,864,256]{2,1,0:T(8,128)(2,1)}, bf16[4,864,256]{2,1,0:T(8,128)(2,1)}) custom-call(s32[5]{0:T(128)} %stack.23.refs_0_.sc, bf16[432,1024]{1,0:T(8,128)(2,1)} %gate.1.refs_0_.refs_8_, bf16[432,1024]{1,0:T(8,128)(2,1)} %collective-permute-done.20.refs_1_.refs_9_, bf16[4,528,256]{2,1,0:T(8,128)(2,1)} %get-tuple-element.125.refs_2_.refs_4_, ...), custom_call_target="tpu_custom_call" | custom-call | bytes 7471104 | tf_op jit(solution)/shard_map/feed_forward_far/pallas_call | solution.py:114
  164.4 8.8 %feed_back.1 = (bf16[4,864,256]{2,1,0:T(8,128)(2,1)}, f32[4,256]{1,0:T(4,128)}, bf16[432,1024]{1,0:T(8,128)(2,1)}, bf16[432,1024]{1,0:T(8,128)(2,1)}) custom-call(s32[5]{0:T(128)} %stack.23.refs_0_.sc, bf16[432,1024]{1,0:T(8,128)(2,1)} %get-tuple-element.126.refs_0_, bf16[432,1024]{1,0:T(8,128)(2,1)} %collective-permute-done.18.refs_1_, ...), custom_call_target="tpu_custom_call" | custom-call | bytes 11341824 | tf_op jit(solution)/shard_map/feed_back/pallas_call | solution.py:114
  173.3 9.0 %feed_back_far.1 = (bf16[4,864,256]{2,1,0:T(8,128)(2,1)}, f32[4,256]{1,0:T(4,128)}, bf16[432,1024]{1,0:T(8,128)(2,1)}, bf16[432,1024]{1,0:T(8,128)(2,1)}) custom-call(s32[5]{0:T(128)} %stack.23.refs_0_.sc, bf16[432,1024]{1,0:T(8,128)(2,1)} %get-tuple-element.137.refs_0_.refs_2_, bf16[432,1024]{1,0:T(8,128)(2,1)} %collective-permute-done.22.refs_1_.refs_3_, ...), custom_call_target="tpu_custom_call" | custom-call | bytes 11341824 | tf_op jit(solution)/shard_map/feed_back_far/pallas_call | solution.py:114
  183.0 2.3 collective-permute-done.23.refs_1_
  185.3 2.9 add.134.refs_12_
  189.2 14.5 %hidden_grad.1 = (bf16[4,1024,256]{2,1,0:T(8,128)(2,1)}, bf16[4,512,256]{2,1,0:T(8,128)(2,1)}, bf16[4,512,256]{2,1,0:T(8,128)(2,1)}) custom-call(s32[5]{0:T(128)} %stack.23.refs_0_.sc, bf16[432,1024]{1,0:T(8,128)(2,1)} %get-tuple-element.126.refs_0_, bf16[432,1024]{1,0:T(8,128)(2,1)} %collective-permute-done.18.refs_1_, ...), custom_call_target="tpu_custom_call" | custom-call | bytes 18350080 | tf_op jit(solution)/shard_map/hidden_grad/pallas_call | solution.py:114
  205.4 6.0 %feed_out_far.1 = (bf16[432,1024]{1,0:T(8,128)(2,1)}, bf16[432,1024]{1,0:T(8,128)(2,1)}) custom-call(s32[5]{0:T(128)} %stack.23.refs_0_.sc, bf16[4,864,256]{2,1,0:T(8,128)(2,1)} %get-tuple-element.134.refs_6_.refs_5_.refs_0_, bf16[4,1024,256]{2,1,0:T(8,128)(2,1)} %bitcast.19, bf16[4,512,256]{2,1,0:T(8,128)(2,1)} %get-tuple-element.143.refs_2_.refs_12_), custom_call_target="tpu_custom_call" | custom-call | bytes 5636096 | tf_op jit(solution)/shard_map/feed_out_far/pallas_call | solution.py:114
  211.5 15.2 %collective-permute-done.24.refs_5_ = bf16[432,1024]{1,0:T(8,128)(2,1)} collective-permute-done((bf16[432,1024]{1,0:T(8,128)(2,1)S(1)}, bf16[432,1024]{1,0:T(8,128)(2,1)}, u32[]{:S(2)}, u32[]{:S(2)}) %collective-permute-start.24) | collective-permute-done | bytes 884768 | tf_op jit(solution)/shard_map/ppermute | solution.py:941
  226.6 7.1 %second_norm_back.1 = (f32[432,1024]{1,0:T(8,128)}, bf16[432,1024]{1,0:T(8,128)(2,1)}, f32[4,1024]{1,0:T(4,128)}) custom-call(s32[5]{0:T(128)} %stack.23.refs_0_.sc, f32[432,1024]{1,0:T(8,128)} %get-tuple-element.129.refs_0_, f32[432,1024]{1,0:T(8,128)} %refs_1_.10, f32[6,1024]{1,0:T(8,128)} %refs_1_.11, bf16[432,1024]{1,0:T(8,128)(2,1)} %get-tuple-element.135.refs_3_, ...), custom_call_target="tpu_custom_call" | custom-call | bytes 7962624 | tf_op jit(solution)/shard_map/second_norm_back/pallas_call | solution.py:50
  234.6 1.9 collective-permute-done.25.refs_1_.refs_6_
  237.3 4.6 %mixed_grad.1 = (bf16[4,864,128]{2,1,0:T(8,128)(2,1)}, bf16[2,288,128]{2,1,0:T(8,128)(2,1)}, bf16[432,1024]{1,0:T(8,128)(2,1)}) custom-call(s32[5]{0:T(128)} %stack.23.refs_0_.sc, bf16[432,1024]{1,0:T(8,128)(2,1)} %get-tuple-element.145.refs_0_.refs_5_, bf16[432,1024]{1,0:T(8,128)(2,1)} %copy-done.6, ...), custom_call_target="tpu_custom_call", output_to_operand_aliasing={{2}: (12, {})} | custom-call | bytes 6995968 | tf_op jit(solution)/shard_map/mixed_grad/pallas_call | solution.py:114
  242.0 6.2 %feed_out.1 = (bf16[432,1024]{1,0:T(8,128)(2,1)}, bf16[432,1024]{1,0:T(8,128)(2,1)}) custom-call(s32[5]{0:T(128)} %stack.23.refs_0_.sc, bf16[4,864,256]{2,1,0:T(8,128)(2,1)} %get-tuple-element.131.refs_0_.refs_4_, bf16[4,1024,256]{2,1,0:T(8,128)(2,1)} %bitcast.20, bf16[4,864,128]{2,1,0:T(8,128)(2,1)} %get-tuple-element.147.refs_2_.refs_1_), custom_call_target="tpu_custom_call" | custom-call | bytes 5636096 | tf_op jit(solution)/shard_map/feed_out/pallas_call | solution.py:114
  248.1 1.8 collective-permute-start.29
  249.9 2.4 add_convert_fusion.1
  252.8 1.6 collective-permute-done.29.refs_3_
  254.4 8.6 %attend_split_back.1 = (bf16[2,288,384]{2,1,0:T(8,128)(2,1)}, bf16[2,288,384]{2,1,0:T(8,128)(2,1)}) custom-call(s32[5]{0:T(128)} %stack.23.refs_0_.sc, bf16[4,864,384]{2,1,0:T(8,128)(2,1)} %get-tuple-element.120.refs_0_, bf16[2,288,384]{2,1,0:T(8,128)(2,1)} %collective-permute-done.12.refs_1_, bf16[4,864,128]{2,1,0:T(8,128)(2,1)} %get-tuple-element.147.refs_2_.refs_1_, ...), custom_call_target="tpu_custom_call" | custom-call | bytes 3096576 | tf_op jit(solution)/shard_map/attend_split_back/pallas_call | solution.py:50
  263.0 1.7 collective-permute-start.30
  264.8 14.6 %attend_whole_back.1 = (bf16[4,576,384]{2,1,0:T(8,128)(2,1)}, bf16[1024,256]{1,0:T(8,128)(2,1)}) custom-call(s32[5]{0:T(128)} %stack.23.refs_0_.sc, bf16[4,864,384]{2,1,0:T(8,128)(2,1)} %get-tuple-element.120.refs_0_, bf16[4,864,128]{2,1,0:T(8,128)(2,1)} %get-tuple-element.147.refs_2_.refs_1_, ...), custom_call_target="tpu_custom_call", output_to_operand_aliasing={{1}: (4, {})} | custom-call | flops 499999997952 | bytes 6193152 | tf_op jit(solution)/shard_map/attend_whole_back/pallas_call | solution.py:50
  279.4 1.8 fusion.4
  282.6 7.8 %first_back.1 = (bf16[432,1024]{1,0:T(8,128)(2,1)}, bf16[432,1024]{1,0:T(8,128)(2,1)}) custom-call(s32[5]{0:T(128)} %stack.23.refs_0_.sc, bf16[4,576,384]{2,1,0:T(8,128)(2,1)} %get-tuple-element.155.refs_0_.refs_2_, bf16[2,288,384]{2,1,0:T(8,128)(2,1)} %get-tuple-element.153.refs_2_.refs_1_.refs_3_, ...), custom_call_target="tpu_custom_call" | custom-call | bytes 8617984 | tf_op jit(solution)/shard_map/first_back/pallas_call | solution.py:114
  291.3 11.0 %attn_grad.1 = (bf16[2,256,512]{2,1,0:T(8,128)(2,1)}, bf16[2,256,512]{2,1,0:T(8,128)(2,1)}, bf16[2,256,512]{2,1,0:T(8,128)(2,1)}, bf16[2,256,512]{2,1,0:T(8,128)...) custom-call(s32[5]{0:T(128)} %stack.23.refs_0_.sc, ...), custom_call_target="tpu_custom_call", output_to_operand_aliasing={{8}: (13, {}), {9}: (14, {})} | custom-call | bytes 11272192 | tf_op jit(solution)/shard_map/attn_grad/pallas_call | solution.py:114
  302.3 2.8 add_convert_fusion
  307.0 6.3 %first_norm_back.1 = (f32[432,1024]{1,0:T(8,128)}, f32[2,1024]{1,0:T(2,128)}) custom-call(s32[5]{0:T(128)} %stack.23.refs_0_.sc, f32[432,1024]{1,0:T(8,128)} %refs_0_.5, f32[432,1024]{1,0:T(8,128)} %get-tuple-element.151.refs_1_, f32[6,1024]{1,0:T(8,128)} %refs_1_.11, bf16[432,1024]{1,0:T(8,128)(2,1)} %get-tuple-element.157.refs_10_.refs_3_, ...), custom_call_target="tpu_custom_call" | custom-call | bytes 7077888 | tf_op jit(solution)/shard_map/first_norm_back/pallas_call | solution.py:50
  315.7 4.2 %collective-permute-done.33.refs_1_ = bf16[2,256,512]{2,1,0:T(8,128)(2,1)} collective-permute-done((bf16[2,256,512]{2,1,0:T(8,128)(2,1)}, bf16[2,256,512]{2,1,0:T(8,128)(2,1)}, u32[]{:S(2)}, u32[]{:S(2)}) %collective-permute-start.33) | collective-permute-done | bytes 524320 | tf_op jit(solution)/shard_map/ppermute | solution.py:941
  321.9 3.0 add.135
  329.6 2.7 collective-permute-done.42
  332.4 3.1 collective-permute-start.41
  335.5 2.5 collective-permute-done.41
  338.6 1.9 collective-permute-start.40
  340.5 5.4 %layer_output.1.refs_6_ = f32[432,1024]{1,0:T(8,128)} custom-call(s32[5]{0:T(128)} %stack.23.refs_0_.sc, f32[432,1024]{1,0:T(8,128)} %get-tuple-element.129.refs_0_, f32[6,1024]{1,0:T(8,128)} %refs_1_.11, bf16[432,1024]{1,0:T(8,128)(2,1)} %get-tuple-element.148.refs_4_.refs_2_, bf16[432,1024]{1,0:T(8,128)(2,1)} %copy-done.14, ...), custom_call_target="tpu_custom_call" | custom-call | bytes 5308416 | tf_op jit(solution)/shard_map/layer_output/pallas_call | solution.py:50
  347.6 3.6 add.136
  355.0 3.3 collective-permute-start.47
  363.0 4.0 %collective-permute-done.50.refs_3_ = bf16[512,256]{1,0:T(8,128)(2,1)S(1)} collective-permute-done((bf16[512,256]{1,0:T(8,128)(2,1)S(1)}, bf16[512,256]{1,0:T(8,128)(2,1)S(1)}, u32[]{:S(2)}, u32[]{:S(2)}) %collective-permute-start.50) | collective-permute-done | bytes 262176 | tf_op jit(solution)/shard_map/ppermute | solution.py:941
  367.7 4.6 %hidden_adam.1 = (f32[256,512]{1,0:T(8,128)}, f32[256,512]{1,0:T(8,128)}, f32[256,512]{1,0:T(8,128)}, f32[256,512]{1,0:T(8,128)}, f32[512,256]{1,0:T(8,128)}, /*...) custom-call(s32[5]{0:T(128)} %stack.23.refs_0_.sc, bf16[512,256]{1,0:T(8,128)(2,1)} %bitcast.22, ...), custom_call_target="tpu_custom_call" | custom-call | bytes 8126484 | tf_op jit(solution)/shard_map/hidden_adam/pallas_call | solution.py:841
  372.5 4.9 %collective-permute-done.48.refs_4_ = bf16[256,512]{1,0:T(8,128)(2,1)} collective-permute-done((bf16[256,512]{1,0:T(8,128)(2,1)}, bf16[256,512]{1,0:T(8,128)(2,1)}, u32[]{:S(2)}, u32[]{:S(2)}) %collective-permute-start.48) | collective-permute-done | bytes 262176 | tf_op jit(solution)/shard_map/ppermute | solution.py:941
  377.4 3.4 attn_adam.1
  (180 shorter events, 50.8 us)
Async XLA Ops:
  7.2 74.5 %all-gather.5.cloned.1.call-start = ((), (), s32[]{:S(2)}) async-start(), calls=%async_computation.4 | async-start | bytes 1351680 | tf_op jit(solution)/shard_map/all_gather | solution.py:944
  9.9 14.2 %copy-start.10 = (bf16[256,512]{1,0:T(8,128)(2,1)S(1)}, bf16[256,512]{1,0:T(8,128)(2,1)}, u32[]{:S(2)}) copy-start(bf16[256,512]{1,0:T(8,128)(2,1)} %attn_piece.1.refs_4_.refs_0_) | copy-start | bytes 786436
  12.0 8.3 %collective-permute-start.3 = (bf16[512,256]{1,0:T(8,128)(2,1)}, bf16[512,256]{1,0:T(8,128)(2,1)S(1)}, u32[]{:S(2)}, u32[]{:S(2)}) collective-permute-start(bf16[512,256]{1,0:T(8,128)(2,1)} %get-tuple-element.114), channel_id=1, source_target_pairs={{0,8},{1,9},{2,10},{3,11},{4,12},{5,13},{6,14},{7,15},{8,0},{9,1},... | collective-permute-start | bytes 786440 | tf_op jit(solution)/shard_map/ppermute | solution.py:941
  12.5 14.4 %collective-permute-start.2 = (bf16[256,512]{1,0:T(8,128)(2,1)}, bf16[256,512]{1,0:T(8,128)(2,1)S(1)}, u32[]{:S(2)}, u32[]{:S(2)}) collective-permute-start(bf16[256,512]{1,0:T(8,128)(2,1)} %attn_piece.1.refs_4_.refs_0_), channel_id=1, source_target_pairs={{0,2},{1,3},{2,0},{3,1},{4,6},{5,7},{6,4},{7,5},{8,10},{9,11},{10,... | collective-permute-start | bytes 786440 | tf_op jit(solution)/shard_map/ppermute | solution.py:941
  22.6 10.1 %collective-permute-start.4 = (bf16[512,256]{1,0:T(8,128)(2,1)}, bf16[512,256]{1,0:T(8,128)(2,1)}, u32[]{:S(2)}, u32[]{:S(2)}) collective-permute-start(bf16[512,256]{1,0:T(8,128)(2,1)} %pad_maximum_fusion.2), channel_id=1, source_target_pairs={{0,16},{1,17},{2,18},{3,19},{4,20},{5,21},{6,22},{7,23},{8,24},{9,... | collective-permute-start | bytes 786440 | tf_op jit(solution)/shard_map/ppermute | solution.py:941
  24.1 19.3 %collective-permute-start.1 = (bf16[256,512]{1,0:T(8,128)(2,1)S(1)}, bf16[256,512]{1,0:T(8,128)(2,1)}, u32[]{:S(2)}, u32[]{:S(2)}) collective-permute-start(bf16[256,512]{1,0:T(8,128)(2,1)S(1)} %copy-done.10), channel_id=1, source_target_pairs={{0,6},{1,7},{2,4},{3,5},{4,2},{5,3},{6,0},{7,1},{8,14},{9,15},{10,... | collective-permute-start | bytes 786440 | tf_op jit(solution)/shard_map/ppermute | solution.py:941
  25.7 21.3 %collective-permute-start = (bf16[256,512]{1,0:T(8,128)(2,1)S(1)}, bf16[256,512]{1,0:T(8,128)(2,1)}, u32[]{:S(2)}, u32[]{:S(2)}) collective-permute-start(bf16[256,512]{1,0:T(8,128)(2,1)S(1)} %copy-done.10), channel_id=1, source_target_pairs={{0,4},{1,5},{2,6},{3,7},{4,0},{5,1},{6,2},{7,3},{8,12},{9,13},{10,... | collective-permute-start | bytes 786440 | tf_op jit(solution)/shard_map/ppermute | solution.py:941
  30.0 20.0 %collective-permute-start.6 = (bf16[2,256,512]{2,1,0:T(8,128)(2,1)}, bf16[2,256,512]{2,1,0:T(8,128)(2,1)S(1)}, u32[]{:S(2)}, u32[]{:S(2)}) collective-permute-start(bf16[2,256,512]{2,1,0:T(8,128)(2,1)} %pack.2.refs_2_.refs_3_), channel_id=1, source_target_pairs={{0,16},{1,17},{2,18},{3,19},{4,20},{5,21},{6,22},{7,23},{8,24},{9,... | collective-permute-start | bytes 1572872 | tf_op jit(solution)/shard_map/ppermute | solution.py:941
  30.6 19.4 %collective-permute-start.5 = (bf16[2,256,512]{2,1,0:T(8,128)(2,1)}, bf16[2,256,512]{2,1,0:T(8,128)(2,1)}, u32[]{:S(2)}, u32[]{:S(2)}) collective-permute-start(bf16[2,256,512]{2,1,0:T(8,128)(2,1)} %pack.2.refs_2_.refs_3_), channel_id=1, source_target_pairs={{0,8},{1,9},{2,10},{3,11},{4,12},{5,13},{6,14},{7,15},{8,0},{9,1},... | collective-permute-start | bytes 1572872 | tf_op jit(solution)/shard_map/ppermute | solution.py:941
  49.4 115.0 %all-gather.7.cloned.1.call-start = ((), (), s32[]{:S(2)}) async-start(), calls=%async_computation.5 | async-start | bytes 2621440 | tf_op jit(solution)/shard_map/all_gather | solution.py:944
  49.4 14.3 %collective-permute-start.9 = (bf16[2,256,512]{2,1,0:T(8,128)(2,1)}, bf16[2,256,512]{2,1,0:T(8,128)(2,1)}, u32[]{:S(2)}, u32[]{:S(2)}) collective-permute-start(bf16[2,256,512]{2,1,0:T(8,128)(2,1)} %get-tuple-element.116.refs_3_.refs_4_), channel_id=1, source_target_pairs={{0,16},{1,17},{2,18},{3,19},{4,20},{5,21},{6,22},{7,23},{8,24},{9,... | collective-permute-start | bytes 1572872 | tf_op jit(solution)/shard_map/ppermute | solution.py:941
  55.8 25.9 %collective-permute-start.7 = (bf16[432,1024]{1,0:T(8,128)(2,1)}, bf16[432,1024]{1,0:T(8,128)(2,1)}, u32[]{:S(2)}, u32[]{:S(2)}) collective-permute-start(bf16[432,1024]{1,0:T(8,128)(2,1)} %get-tuple-element.117.refs_0_), channel_id=1, source_target_pairs={{0,1},{1,0},{2,3},{3,2},{4,5},{5,4},{6,7},{7,6},{8,9},{9,8},{10,11... | collective-permute-start | bytes 2654216 | tf_op jit(solution)/shard_map/ppermute | solution.py:941
  55.9 15.0 %collective-permute-start.8 = (bf16[2,256,512]{2,1,0:T(8,128)(2,1)}, bf16[2,256,512]{2,1,0:T(8,128)(2,1)S(1)}, u32[]{:S(2)}, u32[]{:S(2)}) collective-permute-start(bf16[2,256,512]{2,1,0:T(8,128)(2,1)} %get-tuple-element.116.refs_3_.refs_4_), channel_id=1, source_target_pairs={{0,8},{1,9},{2,10},{3,11},{4,12},{5,13},{6,14},{7,15},{8,0},{9,1},... | collective-permute-start | bytes 1572872 | tf_op jit(solution)/shard_map/ppermute | solution.py:941
  56.4 16.5 %collective-permute-start.10 = (bf16[2,256,512]{2,1,0:T(8,128)(2,1)}, bf16[2,256,512]{2,1,0:T(8,128)(2,1)}, u32[]{:S(2)}, u32[]{:S(2)}) collective-permute-start(bf16[2,256,512]{2,1,0:T(8,128)(2,1)} %collective-permute-done.5.refs_4_.refs_5_), channel_id=1, source_target_pairs={{0,16},{1,17},{2,18},{3,19},{4,20},{5,21},{6,22},{7,23},{8,24},{9,... | collective-permute-start | bytes 1572872 | tf_op jit(solution)/shard_map/ppermute | solution.py:941
  63.8 18.0 %collective-permute-start.11 = (bf16[2,256,512]{2,1,0:T(8,128)(2,1)}, bf16[2,256,512]{2,1,0:T(8,128)(2,1)}, u32[]{:S(2)}, u32[]{:S(2)}) collective-permute-start(bf16[2,256,512]{2,1,0:T(8,128)(2,1)} %collective-permute-done.9.refs_7_.refs_8_), channel_id=1, source_target_pairs={{0,8},{1,9},{2,10},{3,11},{4,12},{5,13},{6,14},{7,15},{8,0},{9,1},... | collective-permute-start | bytes 1572872 | tf_op jit(solution)/shard_map/ppermute | solution.py:941
  70.9 10.9 %copy-start.1 = (bf16[2,256,512]{2,1,0:T(8,128)(2,1)}, bf16[2,256,512]{2,1,0:T(8,128)(2,1)S(1)}, u32[]{:S(2)}) copy-start(bf16[2,256,512]{2,1,0:T(8,128)(2,1)S(1)} %collective-permute-done.8.refs_5_.refs_6_) | copy-start | bytes 1572868
  89.2 25.8 %collective-permute-start.14 = (bf16[4,528,256]{2,1,0:T(8,128)(2,1)}, bf16[4,528,256]{2,1,0:T(8,128)(2,1)}, u32[]{:S(2)}, u32[]{:S(2)}) collective-permute-start(bf16[4,528,256]{2,1,0:T(8,128)(2,1)} %get-tuple-element.125.refs_2_.refs_4_), channel_id=1, source_target_pairs={{0,16},{1,17},{2,18},{3,19},{4,20},{5,21},{6,22},{7,23},{8,24},{9,... | collective-permute-start | bytes 3244040 | tf_op jit(solution)/shard_map/ppermute | solution.py:941
  90.7 12.5 %collective-permute-start.12 = (bf16[2,288,384]{2,1,0:T(8,128)(2,1)}, bf16[2,288,384]{2,1,0:T(8,128)(2,1)}, u32[]{:S(2)}, u32[]{:S(2)}) collective-permute-start(bf16[2,288,384]{2,1,0:T(8,128)(2,1)} %get-tuple-element.121), channel_id=1, source_target_pairs={{0,2},{1,3},{2,0},{3,1},{4,6},{5,7},{6,4},{7,5},{8,10},{9,11},{10,... | collective-permute-start | bytes 1327112 | tf_op jit(solution)/shard_map/ppermute | solution.py:941
  93.2 21.0 %collective-permute-start.15 = (bf16[432,1024]{1,0:T(8,128)(2,1)}, bf16[432,1024]{1,0:T(8,128)(2,1)S(1)}, u32[]{:S(2)}, u32[]{:S(2)}) collective-permute-start(bf16[432,1024]{1,0:T(8,128)(2,1)} %get-tuple-element.126.refs_0_), channel_id=1, source_target_pairs={{0,8},{1,9},{2,10},{3,11},{4,12},{5,13},{6,14},{7,15},{8,0},{9,1},... | collective-permute-start | bytes 2654216 | tf_op jit(solution)/shard_map/ppermute | solution.py:941
  108.7 156.1 %reduce-scatter.3.cloned.1.call-start = ((), (), s32[]{:S(2)}) async-start(), calls=%async_computation.2 | async-start | bytes 2621440 | tf_op jit(solution)/shard_map/reduce_scatter | solution.py:947
  108.7 5.4 %collective-permute-start.13 = (bf16[2,288,128]{2,1,0:T(8,128)(2,1)}, bf16[2,288,128]{2,1,0:T(8,128)(2,1)S(1)}, u32[]{:S(2)}, u32[]{:S(2)}) collective-permute-start(bf16[2,288,128]{2,1,0:T(8,128)(2,1)} %get-tuple-element.124), channel_id=1, source_target_pairs={{0,2},{1,3},{2,0},{3,1},{4,6},{5,7},{6,4},{7,5},{8,10},{9,11},{10,... | collective-permute-start | bytes 442376 | tf_op jit(solution)/shard_map/ppermute | solution.py:941
  120.7 2.7 collective-permute-start.16
  129.9 2.8 collective-permute-start.17
  130.2 22.1 %collective-permute-start.19 = (bf16[432,1024]{1,0:T(8,128)(2,1)}, bf16[432,1024]{1,0:T(8,128)(2,1)S(1)}, u32[]{:S(2)}, u32[]{:S(2)}) collective-permute-start(bf16[432,1024]{1,0:T(8,128)(2,1)} %get-tuple-element.130.refs_0_.refs_6_), channel_id=1, source_target_pairs={{0,8},{1,9},{2,10},{3,11},{4,12},{5,13},{6,14},{7,15},{8,0},{9,1},... | collective-permute-start | bytes 2654216 | tf_op jit(solution)/shard_map/ppermute | solution.py:941
  154.0 2.8 collective-permute-start.20
  154.1 10.3 %collective-permute-start.18 = (bf16[432,1024]{1,0:T(8,128)(2,1)}, bf16[432,1024]{1,0:T(8,128)(2,1)}, u32[]{:S(2)}, u32[]{:S(2)}) collective-permute-start(bf16[432,1024]{1,0:T(8,128)(2,1)} %get-tuple-element.126.refs_0_), channel_id=1, source_target_pairs={{0,1},{1,0},{2,3},{3,2},{4,5},{5,4},{6,7},{7,6},{8,9},{9,8},{10,11... | collective-permute-start | bytes 2654216 | tf_op jit(solution)/shard_map/ppermute | solution.py:941
  154.6 18.6 %collective-permute-start.22 = (bf16[432,1024]{1,0:T(8,128)(2,1)S(1)}, bf16[432,1024]{1,0:T(8,128)(2,1)}, u32[]{:S(2)}, u32[]{:S(2)}) collective-permute-start(bf16[432,1024]{1,0:T(8,128)(2,1)S(1)} %copy-done.3), channel_id=1, source_target_pairs={{0,1},{1,0},{2,3},{3,2},{4,5},{5,4},{6,7},{7,6},{8,9},{9,8},{10,11... | collective-permute-start | bytes 2654216 | tf_op jit(solution)/shard_map/ppermute | solution.py:941
  182.3 3.0 collective-permute-start.23
  182.6 5.6 %collective-permute-start.21 = (bf16[432,1024]{1,0:T(8,128)(2,1)}, bf16[432,1024]{1,0:T(8,128)(2,1)S(1)}, u32[]{:S(2)}, u32[]{:S(2)}) collective-permute-start(bf16[432,1024]{1,0:T(8,128)(2,1)} %get-tuple-element.136), channel_id=1, source_target_pairs={{0,1},{1,0},{2,3},{3,2},{4,5},{5,4},{6,7},{7,6},{8,9},{9,8},{10,11... | collective-permute-start | bytes 2654216 | tf_op jit(solution)/shard_map/ppermute | solution.py:941
  203.7 155.9 %reduce-scatter.5.cloned.1.call-start = ((), (), s32[]{:S(2)}) async-start(), calls=%async_computation.3 | async-start | bytes 1310720 | tf_op jit(solution)/shard_map/reduce_scatter | solution.py:947
  204.8 21.8 %collective-permute-start.24 = (bf16[432,1024]{1,0:T(8,128)(2,1)S(1)}, bf16[432,1024]{1,0:T(8,128)(2,1)}, u32[]{:S(2)}, u32[]{:S(2)}) collective-permute-start(bf16[432,1024]{1,0:T(8,128)(2,1)S(1)} %copy-done.8), channel_id=1, source_target_pairs={{0,8},{1,9},{2,10},{3,11},{4,12},{5,13},{6,14},{7,15},{8,0},{9,1},... | collective-permute-start | bytes 2654216 | tf_op jit(solution)/shard_map/ppermute | solution.py:941
  211.4 23.2 %collective-permute-start.26 = (bf16[432,1024]{1,0:T(8,128)(2,1)}, bf16[432,1024]{1,0:T(8,128)(2,1)}, u32[]{:S(2)}, u32[]{:S(2)}) collective-permute-start(bf16[432,1024]{1,0:T(8,128)(2,1)} %get-tuple-element.146), channel_id=1, source_target_pairs={{0,1},{1,0},{2,3},{3,2},{4,5},{5,4},{6,7},{7,6},{8,9},{9,8},{10,11... | collective-permute-start | bytes 2654216 | tf_op jit(solution)/shard_map/ppermute | solution.py:941
  233.7 2.7 collective-permute-start.25
  233.8 68.5 %collective-permute-start.49 = (bf16[4,512,256]{2,1,0:T(8,128)(2,1)}, bf16[4,512,256]{2,1,0:T(8,128)(2,1)}, u32[]{:S(2)}, u32[]{:S(2)}) collective-permute-start(bf16[4,512,256]{2,1,0:T(8,128)(2,1)} %get-tuple-element.182), channel_id=1, source_target_pairs={{0,16},{1,17},{2,18},{3,19},{4,20},{5,21},{6,22},{7,23},{8,24},{9,... | collective-permute-start | bytes 3145736 | tf_op jit(solution)/shard_map/ppermute | solution.py:941
  248.1 6.3 %collective-permute-start.29 = (bf16[2,288,128]{2,1,0:T(8,128)(2,1)}, bf16[2,288,128]{2,1,0:T(8,128)(2,1)}, u32[]{:S(2)}, u32[]{:S(2)}) collective-permute-start(bf16[2,288,128]{2,1,0:T(8,128)(2,1)} %get-tuple-element.152), channel_id=1, source_target_pairs={{0,2},{1,3},{2,0},{3,1},{4,6},{5,7},{6,4},{7,5},{8,10},{9,11},{10,... | collective-permute-start | bytes 442376 | tf_op jit(solution)/shard_map/ppermute | solution.py:941
  252.3 30.3 %collective-permute-start.28 = (bf16[432,1024]{1,0:T(8,128)(2,1)}, bf16[432,1024]{1,0:T(8,128)(2,1)}, u32[]{:S(2)}, u32[]{:S(2)}) collective-permute-start(bf16[432,1024]{1,0:T(8,128)(2,1)} %add_convert_fusion.1), channel_id=1, source_target_pairs={{0,8},{1,9},{2,10},{3,11},{4,12},{5,13},{6,14},{7,15},{8,0},{9,1},... | collective-permute-start | bytes 2654216 | tf_op jit(solution)/shard_map/ppermute | solution.py:941
  263.0 19.6 %collective-permute-start.30 = (bf16[2,288,384]{2,1,0:T(8,128)(2,1)}, bf16[2,288,384]{2,1,0:T(8,128)(2,1)}, u32[]{:S(2)}, u32[]{:S(2)}) collective-permute-start(bf16[2,288,384]{2,1,0:T(8,128)(2,1)} %get-tuple-element.156), channel_id=1, source_target_pairs={{0,2},{1,3},{2,0},{3,1},{4,6},{5,7},{6,4},{7,5},{8,10},{9,11},{10,... | collective-permute-start | bytes 1327112 | tf_op jit(solution)/shard_map/ppermute | solution.py:941
  281.2 9.4 %collective-permute-start.32 = (bf16[512,256]{1,0:T(8,128)(2,1)S(1)}, bf16[512,256]{1,0:T(8,128)(2,1)S(1)}, u32[]{:S(2)}, u32[]{:S(2)}) collective-permute-start(bf16[512,256]{1,0:T(8,128)(2,1)S(1)} %get-tuple-element.209), channel_id=1, source_target_pairs={{0,16},{1,17},{2,18},{3,19},{4,20},{5,21},{6,22},{7,23},{8,24},{9,... | collective-permute-start | bytes 786440 | tf_op jit(solution)/shard_map/ppermute | solution.py:941
  290.5 16.5 %collective-permute-start.31 = (bf16[432,1024]{1,0:T(8,128)(2,1)}, bf16[432,1024]{1,0:T(8,128)(2,1)}, u32[]{:S(2)}, u32[]{:S(2)}) collective-permute-start(bf16[432,1024]{1,0:T(8,128)(2,1)} %get-tuple-element.158), channel_id=1, source_target_pairs={{0,1},{1,0},{2,3},{3,2},{4,5},{5,4},{6,7},{7,6},{8,9},{9,8},{10,11... | collective-permute-start | bytes 2654216 | tf_op jit(solution)/shard_map/ppermute | solution.py:941
  305.1 22.9 %collective-permute-start.27 = (bf16[432,1024]{1,0:T(8,128)(2,1)}, bf16[432,1024]{1,0:T(8,128)(2,1)S(1)}, u32[]{:S(2)}, u32[]{:S(2)}) collective-permute-start(bf16[432,1024]{1,0:T(8,128)(2,1)} %get-tuple-element.149), channel_id=1, source_target_pairs={{0,1},{1,0},{2,3},{3,2},{4,5},{5,4},{6,7},{7,6},{8,9},{9,8},{10,11... | collective-permute-start | bytes 2654216 | tf_op jit(solution)/shard_map/ppermute | solution.py:941
  305.6 14.2 %collective-permute-start.33 = (bf16[2,256,512]{2,1,0:T(8,128)(2,1)}, bf16[2,256,512]{2,1,0:T(8,128)(2,1)}, u32[]{:S(2)}, u32[]{:S(2)}) collective-permute-start(bf16[2,256,512]{2,1,0:T(8,128)(2,1)} %get-tuple-element.164), channel_id=1, source_target_pairs={{0,8},{1,9},{2,10},{3,11},{4,12},{5,13},{6,14},{7,15},{8,0},{9,1},... | collective-permute-start | bytes 1572872 | tf_op jit(solution)/shard_map/ppermute | solution.py:941
  306.2 15.1 %collective-permute-start.34 = (bf16[2,256,512]{2,1,0:T(8,128)(2,1)}, bf16[2,256,512]{2,1,0:T(8,128)(2,1)}, u32[]{:S(2)}, u32[]{:S(2)}) collective-permute-start(bf16[2,256,512]{2,1,0:T(8,128)(2,1)} %get-tuple-element.166), channel_id=1, source_target_pairs={{0,16},{1,17},{2,18},{3,19},{4,20},{5,21},{6,22},{7,23},{8,24},{9,... | collective-permute-start | bytes 1572872 | tf_op jit(solution)/shard_map/ppermute | solution.py:941
  314.0 7.3 %collective-permute-start.35 = (f32[10,1024]{1,0:T(8,128)S(1)}, f32[10,1024]{1,0:T(8,128)S(1)}, u32[]{:S(2)}, u32[]{:S(2)}) collective-permute-start(f32[10,1024]{1,0:T(8,128)S(1)} %pad_maximum_fusion.4.refs_5_), channel_id=1, source_target_pairs={{0,1},{1,0},{2,3},{3,2},{4,5},{5,4},{6,7},{7,6},{8,9},{9,8},{10,11... | collective-permute-start | bytes 122888 | tf_op jit(solution)/shard_map/ppermute | solution.py:941
  314.1 33.4 %collective-permute-start.37 = (bf16[2,256,512]{2,1,0:T(8,128)(2,1)}, bf16[2,256,512]{2,1,0:T(8,128)(2,1)}, u32[]{:S(2)}, u32[]{:S(2)}) collective-permute-start(bf16[2,256,512]{2,1,0:T(8,128)(2,1)} %get-tuple-element.173), channel_id=1, source_target_pairs={{0,16},{1,17},{2,18},{3,19},{4,20},{5,21},{6,22},{7,23},{8,24},{9,... | collective-permute-start | bytes 1572872 | tf_op jit(solution)/shard_map/ppermute | solution.py:941
  319.9 27.7 %collective-permute-start.38 = (bf16[2,256,512]{2,1,0:T(8,128)(2,1)}, bf16[2,256,512]{2,1,0:T(8,128)(2,1)}, u32[]{:S(2)}, u32[]{:S(2)}) collective-permute-start(bf16[2,256,512]{2,1,0:T(8,128)(2,1)} %get-tuple-element.174), channel_id=1, source_target_pairs={{0,8},{1,9},{2,10},{3,11},{4,12},{5,13},{6,14},{7,15},{8,0},{9,1},... | collective-permute-start | bytes 1572872 | tf_op jit(solution)/shard_map/ppermute | solution.py:941
  325.0 22.5 %collective-permute-start.36 = (bf16[2,256,512]{2,1,0:T(8,128)(2,1)}, bf16[2,256,512]{2,1,0:T(8,128)(2,1)}, u32[]{:S(2)}, u32[]{:S(2)}) collective-permute-start(bf16[2,256,512]{2,1,0:T(8,128)(2,1)} %get-tuple-element.172), channel_id=1, source_target_pairs={{0,8},{1,9},{2,10},{3,11},{4,12},{5,13},{6,14},{7,15},{8,0},{9,1},... | collective-permute-start | bytes 1572872 | tf_op jit(solution)/shard_map/ppermute | solution.py:941
  326.5 21.0 %collective-permute-start.39 = (bf16[2,256,512]{2,1,0:T(8,128)(2,1)}, bf16[2,256,512]{2,1,0:T(8,128)(2,1)}, u32[]{:S(2)}, u32[]{:S(2)}) collective-permute-start(bf16[2,256,512]{2,1,0:T(8,128)(2,1)} %get-tuple-element.175), channel_id=1, source_target_pairs={{0,16},{1,17},{2,18},{3,19},{4,20},{5,21},{6,22},{7,23},{8,24},{9,... | collective-permute-start | bytes 1572872 | tf_op jit(solution)/shard_map/ppermute | solution.py:941
  328.0 12.5 %copy-start.17 = (f32[10,1024]{1,0:T(8,128)}, f32[10,1024]{1,0:T(8,128)S(1)}, u32[]{:S(2)}) copy-start(f32[10,1024]{1,0:T(8,128)S(1)} %add.89.refs_7_) | copy-start | bytes 122884
  328.0 12.5 %copy-start.14 = (bf16[432,1024]{1,0:T(8,128)(2,1)}, bf16[432,1024]{1,0:T(8,128)(2,1)S(1)}, u32[]{:S(2)}) copy-start(bf16[432,1024]{1,0:T(8,128)(2,1)S(1)} %collective-permute-done.27.refs_3_) | copy-start | bytes 2654212
  328.0 4.3 %collective-permute-start.42 = (f32[10,1024]{1,0:T(8,128)S(1)}, f32[10,1024]{1,0:T(8,128)S(1)}, u32[]{:S(2)}, u32[]{:S(2)}) collective-permute-start(f32[10,1024]{1,0:T(8,128)S(1)} %add.89.refs_7_), channel_id=1, source_target_pairs={{0,6},{1,7},{2,4},{3,5},{4,2},{5,3},{6,0},{7,1},{8,14},{9,15},{10,... | collective-permute-start | bytes 122888 | tf_op jit(solution)/shard_map/ppermute | solution.py:941
  332.4 5.6 %collective-permute-start.41 = (f32[10,1024]{1,0:T(8,128)S(1)}, f32[10,1024]{1,0:T(8,128)S(1)}, u32[]{:S(2)}, u32[]{:S(2)}) collective-permute-start(f32[10,1024]{1,0:T(8,128)S(1)} %add.89.refs_7_), channel_id=1, source_target_pairs={{0,4},{1,5},{2,6},{3,7},{4,0},{5,1},{6,2},{7,3},{8,12},{9,13},{10,... | collective-permute-start | bytes 122888 | tf_op jit(solution)/shard_map/ppermute | solution.py:941
  338.6 7.3 %collective-permute-start.40 = (f32[10,1024]{1,0:T(8,128)S(1)}, f32[10,1024]{1,0:T(8,128)}, u32[]{:S(2)}, u32[]{:S(2)}) collective-permute-start(f32[10,1024]{1,0:T(8,128)S(1)} %add.89.refs_7_), channel_id=1, source_target_pairs={{0,2},{1,3},{2,0},{3,1},{4,6},{5,7},{6,4},{7,5},{8,10},{9,11},{10,... | collective-permute-start | bytes 122888 | tf_op jit(solution)/shard_map/ppermute | solution.py:941
  351.1 10.5 %copy-start.29 = (f32[512]{0:T(512)S(1)}, f32[512]{0:T(512)}, u32[]{:S(2)}) copy-start(f32[512]{0:T(512)} %param.34) | copy-start | bytes 6148
  351.2 11.1 %copy-start.16 = (f32[6,1024]{1,0:T(8,128)S(1)}, f32[6,1024]{1,0:T(8,128)}, u32[]{:S(2)}) copy-start(f32[6,1024]{1,0:T(8,128)} %refs_1_.11) | copy-start | bytes 73732
  351.2 11.1 %copy-start.26 = (f32[6,1024]{1,0:T(8,128)S(1)}, f32[6,1024]{1,0:T(8,128)}, u32[]{:S(2)}) copy-start(f32[6,1024]{1,0:T(8,128)} %param.24) | copy-start | bytes 73732
  351.2 11.1 %copy-start.27 = (f32[6,1024]{1,0:T(8,128)S(1)}, f32[6,1024]{1,0:T(8,128)}, u32[]{:S(2)}) copy-start(f32[6,1024]{1,0:T(8,128)} %param.23) | copy-start | bytes 73732
  351.2 7.2 %collective-permute-start.45 = (f32[10,1024]{1,0:T(8,128)}, f32[10,1024]{1,0:T(8,128)S(1)}, u32[]{:S(2)}, u32[]{:S(2)}) collective-permute-start(f32[10,1024]{1,0:T(8,128)} %get-tuple-element.176), channel_id=1, source_target_pairs={{0,24},{1,25},{2,26},{3,27},{4,28},{5,29},{6,30},{7,31},{8,16},{9,... | collective-permute-start | bytes 122888 | tf_op jit(solution)/shard_map/ppermute | solution.py:941
  352.7 6.0 %collective-permute-start.44 = (f32[10,1024]{1,0:T(8,128)}, f32[10,1024]{1,0:T(8,128)S(1)}, u32[]{:S(2)}, u32[]{:S(2)}) collective-permute-start(f32[10,1024]{1,0:T(8,128)} %get-tuple-element.176), channel_id=1, source_target_pairs={{0,16},{1,17},{2,18},{3,19},{4,20},{5,21},{6,22},{7,23},{8,24},{9,... | collective-permute-start | bytes 122888 | tf_op jit(solution)/shard_map/ppermute | solution.py:941
  353.3 5.4 %collective-permute-start.43 = (f32[10,1024]{1,0:T(8,128)}, f32[10,1024]{1,0:T(8,128)S(1)}, u32[]{:S(2)}, u32[]{:S(2)}) collective-permute-start(f32[10,1024]{1,0:T(8,128)} %get-tuple-element.176), channel_id=1, source_target_pairs={{0,8},{1,9},{2,10},{3,11},{4,12},{5,13},{6,14},{7,15},{8,0},{9,1},... | collective-permute-start | bytes 122888 | tf_op jit(solution)/shard_map/ppermute | solution.py:941
  354.8 12.2 %copy-start.11 = (bf16[512,256]{1,0:T(8,128)(2,1)}, bf16[512,256]{1,0:T(8,128)(2,1)S(1)}, u32[]{:S(2)}) copy-start(bf16[512,256]{1,0:T(8,128)(2,1)S(1)} %add_convert_fusion.2.refs_2_) | copy-start | bytes 786436
  354.8 17.4 %collective-permute-start.46 = (bf16[256,512]{1,0:T(8,128)(2,1)}, bf16[256,512]{1,0:T(8,128)(2,1)S(1)}, u32[]{:S(2)}, u32[]{:S(2)}) collective-permute-start(bf16[256,512]{1,0:T(8,128)(2,1)} %get-tuple-element.178), channel_id=1, source_target_pairs={{0,2},{1,3},{2,0},{3,1},{4,6},{5,7},{6,4},{7,5},{8,10},{9,11},{10,... | collective-permute-start | bytes 786440 | tf_op jit(solution)/shard_map/ppermute | solution.py:941
  355.0 17.4 %collective-permute-start.47 = (bf16[256,512]{1,0:T(8,128)(2,1)}, bf16[256,512]{1,0:T(8,128)(2,1)}, u32[]{:S(2)}, u32[]{:S(2)}) collective-permute-start(bf16[256,512]{1,0:T(8,128)(2,1)} %get-tuple-element.179), channel_id=1, source_target_pairs={{0,4},{1,5},{2,6},{3,7},{4,0},{5,1},{6,2},{7,3},{8,12},{9,13},{10,... | collective-permute-start | bytes 786440 | tf_op jit(solution)/shard_map/ppermute | solution.py:941
  358.4 19.0 %collective-permute-start.48 = (bf16[256,512]{1,0:T(8,128)(2,1)}, bf16[256,512]{1,0:T(8,128)(2,1)}, u32[]{:S(2)}, u32[]{:S(2)}) collective-permute-start(bf16[256,512]{1,0:T(8,128)(2,1)} %get-tuple-element.180), channel_id=1, source_target_pairs={{0,6},{1,7},{2,4},{3,5},{4,2},{5,3},{6,0},{7,1},{8,14},{9,15},{10,... | collective-permute-start | bytes 786440 | tf_op jit(solution)/shard_map/ppermute | solution.py:941
  360.5 6.4 %collective-permute-start.50 = (bf16[512,256]{1,0:T(8,128)(2,1)S(1)}, bf16[512,256]{1,0:T(8,128)(2,1)S(1)}, u32[]{:S(2)}, u32[]{:S(2)}) collective-permute-start(bf16[512,256]{1,0:T(8,128)(2,1)S(1)} %pad_maximum_fusion.3), channel_id=1, source_target_pairs={{0,8},{1,9},{2,10},{3,11},{4,12},{5,13},{6,14},{7,15},{8,0},{9,1},... | collective-permute-start | bytes 786440 | tf_op jit(solution)/shard_map/ppermute | solution.py:941
  (25 other events, 89.6 us)
Sparse Core Ops, SparseCore 0:
  49.5 29.4 all-gather.4
  108.8 44.6 all-gather.6
  203.8 42.8 reduce-scatter.2
  305.2 24.7 reduce-scatter.4
